TPU v7x, 128 devices: a whole 4x4x4 slice. The times are simulated.
128 devices in a mesh: dp: 16 (over x, y), mp: 8 (over z, core).
Axes of the slice: x: 4, y: 4, z: 4, core: 2. Of those that a mesh axis runs over, the one named last changes fastest.
Arguments:
- hidden_act: bfloat16 [8192, 14336], P('dp', 'mp'), may hold values from -6 to 6
- cotangent: bfloat16 [8192, 4096], P('dp', 'mp'), may hold values from -6 to 6
- weight: bfloat16 [14336, 4096], P('mp'), may hold values from -0.046875 to 0.046875
- deltas: bfloat16 [512, 16384], P('mp'), may hold values from -0.29882812 to 0.29882812
- block_ids: int32 [512], P('mp'), may hold values from 0 to 447, as said below
- owners: int32 [512, 1], P('mp'), may hold values from 0 to 15; in each aligned block of 64 rows (0 to 63, 64 to 127, ...) at most 8 rows name the same one
- first_moment: float32 [8, 128, 16384], P('mp', 'dp'), may hold values from -6 to 6
- second_moment: float32 [8, 128, 16384], P('mp', 'dp'), may hold values from 0.3 to 3
Outputs:
- input_grad: bfloat16 [8192, 14336], P('dp', 'mp')
- new_deltas: bfloat16 [512, 16384], P('mp')
- new_first: float32 [8, 128, 16384], P('mp', 'dp')
- new_second: float32 [8, 128, 16384], P('mp', 'dp')
Inputs may be any that keep to these rules, and one draw needn't show every extreme that they name: `block_ids`: within one index of mp the 64 entries are distinct local block numbers row * 32 + column, with row below 14; the last number is always among them. `owners`: among the 64 blocks of one index of mp no owner is named more than 8 times, a bound that some block reaches.
All inputs are finite; a program needn't handle non-finite values.
Results may differ from a plain program's by a relative error of at most 0.0048.
Values may be sent and summed in bfloat16 or wider, within the bound.
A program may use at most 192 MiB of HBM per device.

v0:
```python
import math

import jax
import jax.numpy as jnp
from jax import lax
from jax.sharding import PartitionSpec as P

D = 4096
BS = 128


BETA_ONE = 0.9
BETA_TWO = 0.95
LEARN_RATE = 0.02
EPSILON = 1e-08
CORRECT_ONE = 1.0 - 0.9**4
CORRECT_TWO = 1.0 - 0.95**4


def local(hidden_act, cotangent, weight, deltas, block_ids, owners, first_moment, second_moment):
    groups = lax.axis_size("dp")
    tok_rows = hidden_act.shape[0]
    ff_local = hidden_act.shape[1]
    row_blocks = ff_local // BS
    col_blocks = D // BS
    count_blocks = deltas.shape[0]
    capacity = first_moment.shape[1]
    slots_all = groups * capacity
    full_dy = lax.all_gather(cotangent, "mp", axis=1, tiled=True)
    block_rows = block_ids // col_blocks
    block_cols = block_ids % col_blocks
    delta_tiles = deltas.reshape(count_blocks, BS, BS)
    weight_view = weight.reshape(row_blocks, BS, col_blocks, BS)
    merged = weight_view.at[block_rows, :, block_cols, :].add(delta_tiles).reshape(ff_local, D)
    dims = (((1,), (1,)), ((), ()))
    input_grad = lax.dot_general(full_dy, merged, dims, preferred_element_type=jnp.float32).astype(
        jnp.bfloat16
    )
    owner_list = owners[:, 0]
    positions = jnp.arange(count_blocks)
    same_owner = owner_list[:, None] == owner_list[None, :]
    earlier = positions[None, :] < positions[:, None]
    slot_rank = jnp.sum(jnp.where(same_owner & earlier, 1, 0), axis=1).astype(jnp.int32)
    target = owner_list * capacity + slot_rank
    slot_hits = target[None, :] == jnp.arange(slots_all)[:, None]
    slot_block = jnp.sum(jnp.where(slot_hits, positions[None, :], 0), axis=1)
    filled_all = jnp.any(slot_hits, axis=1)
    outer_dims = (((0,), (0,)), ((), ()))
    products = lax.dot_general(hidden_act, full_dy, outer_dims, preferred_element_type=jnp.float32)
    product_view = products.reshape(row_blocks, BS, col_blocks, BS)
    partial_grads = product_view[block_rows, :, block_cols, :].reshape(count_blocks, BS * BS)
    my_index = lax.axis_index("dp")
    start_mine = my_index * capacity
    mine_block = lax.dynamic_slice_in_dim(slot_block, start_mine, capacity)
    mine_filled = lax.dynamic_slice_in_dim(filled_all, start_mine, capacity)
    keep_rows = filled_all.astype(jnp.float32)
    summed = lax.psum_scatter(
        (jnp.take(partial_grads, slot_block, axis=0) * keep_rows[:, None]).astype(jnp.bfloat16),
        "dp",
        scatter_dimension=0,
        tiled=True,
    ).astype(jnp.float32)
    scaled_grad = summed / math.sqrt(tok_rows * groups)
    keep_mask = mine_filled[:, None]
    first_prev = first_moment[0]
    second_prev = second_moment[0]
    first_next = BETA_ONE * first_prev + (1.0 - BETA_ONE) * scaled_grad
    second_next = BETA_TWO * second_prev + (1.0 - BETA_TWO) * scaled_grad * scaled_grad
    current = jnp.take(deltas, mine_block, axis=0).astype(jnp.float32)
    stepped = current - LEARN_RATE * (first_next / CORRECT_ONE) / (
        jnp.sqrt(second_next / CORRECT_TWO) + EPSILON
    )
    stepped = jnp.where(
        keep_mask, stepped.astype(jnp.bfloat16), jnp.zeros_like(stepped, jnp.bfloat16)
    )
    new_first = jnp.where(keep_mask, first_next, first_prev)[None]
    new_second = jnp.where(keep_mask, second_next, second_prev)[None]
    gathered = lax.all_gather(stepped, "dp", axis=0, tiled=True)
    new_deltas = jnp.take(gathered, target, axis=0)
    return (input_grad, new_deltas, new_first, new_second)


def solution(mesh):
    in_specs = (
        P("dp", "mp"),
        P("dp", "mp"),
        P("mp", None),
        P("mp", None),
        P("mp"),
        P("mp", None),
        P("mp", "dp", None),
        P("mp", "dp", None),
    )
    out_specs = (P("dp", "mp"), P("mp", None), P("mp", "dp", None), P("mp", "dp", None))
    return jax.shard_map(local, mesh=mesh, in_specs=in_specs, out_specs=out_specs, check_vma=False)
```

profile of v0, /device:TPU:0, one launch (start us, length us, event | category | flops | bytes accessed | tf_op | source)
XLA Modules:
  0.0 322.1 jit_solution(2172282048808962528)
XLA Ops:
  7.2 0.0 copy-start
  7.2 0.0 all-gather.3.cloned.1.call-start
  7.2 0.7 all-gather.3.cloned.1.call-update
  7.9 0.0 all-reduce.3.cloned.1.call-start
  8.0 0.9 select_reduce_fusion.1
  8.9 0.7 multiply_add_fusion
  9.5 0.1 fusion.18
  9.6 0.1 select_reduce_fusion
  9.8 0.7 fusion.25
  10.4 34.1 %all-gather.3.cloned.1.call-done = bf16[512,4096]{1,0:T(8,128)(2,1)} async-done(((bf16[512,512]{1,0:T(8,128)(2,1)}), bf16[512,4096]{1,0:T(8,128)(2,1)}) %all-gather.3.cloned.1.call-update) | async-done | bytes 4194320 | tf_op jit(solution)/shard_map/all_gather | solution.py:29
  44.5 0.0 copy-done
  44.5 15.8 %convolution_bitcast_fusion = f32[224,8,32,128]{3,1,2,0:T(8,128)} fusion(bf16[512,1792]{1,0:T(8,128)(2,1)S(1)} %copy-done, bf16[512,4096]{1,0:T(8,128)(2,1)} %all-gather.3.cloned.1.call-done), kind=kOutput, calls=%fused_computation.8 | convolution fusion | flops 7516192768 | bytes 35389440 | tf_op jit(solution)/shard_map/dot_general | solution.py:49
  60.3 15.3 %copy.29 = f32[224,8,32,128]{3,2,1,0:T(8,128)S(1)} copy(f32[224,8,32,128]{3,1,2,0:T(8,128)} %convolution_bitcast_fusion) | data formatting | bytes 58720256
  75.6 19.1 %copy.24 = f32[14,128,32,128]{3,1,2,0:T(8,128)} copy(f32[14,128,32,128]{3,2,1,0:T(8,128)S(1)} %bitcast.103) | data formatting | bytes 58720256 | tf_op jit(solution)/shard_map/reshape | solution.py:50
  94.7 12.2 %gather_fusion.1 = f32[64,128,128]{2,1,0:T(8,128)} fusion(f32[14,128,32,128]{3,1,2,0:T(8,128)} %copy.24, s32[64]{0:T(128)S(1)} %get-tuple-element.26), kind=kCustom, calls=%fused_computation.1 | custom fusion | bytes 8389120 | tf_op jit(solution)/shard_map/gather | solution.py:51
  106.9 6.5 %copy.40 = f32[8,8,128,128]{3,1,2,0:T(8,128)} copy(f32[8,8,128,128]{3,2,1,0:T(8,128)} %bitcast.105) | data formatting | bytes 8388608
  113.5 11.8 %gather_fusion.2 = f32[128,16384]{1,0:T(8,128)} fusion(f32[64,16384]{1,0:T(8,128)} %bitcast.102, s32[1024]{0:T(1024)S(1)} %pad_clamp_fusion.1), kind=kCustom, calls=%fused_computation.2 | custom fusion | bytes 16777728 | tf_op jit(solution)/shard_map/jit(_take)/gather | solution.py:58
  125.3 6.2 %multiply_convert_fusion = bf16[128,16384]{1,0:T(8,128)(2,1)} fusion(f32[128,16384]{1,0:T(8,128)} %gather_fusion.2, f32[128]{0:T(128)S(1)} %convert_element_type.28, pred[128]{0:T(512)(128)(4,1)S(1)} %compare_and_fusion), kind=kLoop, calls=%fused_computation.9 | loop fusion | flops 6291456 | bytes 12583552 | tf_op jit(solution)/shard_map/convert_element_type | solution.py:58
  131.5 0.0 copy-start.3
  131.5 0.0 copy-start.4
  131.5 0.0 all-reduce.3.cloned.1.call-update
  131.6 0.0 all-gather.5.cloned.1.call-start
  131.6 0.1 dynamic_slice.6
  131.7 0.1 compare_and_fusion.1
  131.8 2.9 gather_fusion
  134.7 0.0 copy-done.6
  134.7 0.6 dynamic-slice
  135.9 98.9 %all-reduce.3.cloned.1.call-done = bf16[128,16384]{1,0:T(8,128)(2,1)} async-done(((bf16[128,16384]{1,0:T(8,128)(2,1)}), bf16[128,16384]{1,0:T(8,128)(2,1)}) %all-reduce.3.cloned.1.call-update) | async-done | bytes 4194320
  234.8 0.0 copy-done.3
  234.8 0.0 copy-done.4
  234.8 2.1 broadcast_select_fusion.1
  236.9 0.0 all-gather.5.cloned.1.call-update
  236.9 8.9 %copy.26 = bf16[224,8,32,128]{3,2,1,0:T(8,128)(2,1)S(1)} copy(bf16[224,8,32,128]{3,1,2,0:T(8,128)(2,1)} %bitcast.106) | data formatting | bytes 29360128
  245.9 0.0 copy-start.2
  245.9 8.3 %copy.22 = bf16[14,128,32,128]{3,1,2,0:T(8,128)(2,1)} copy(bf16[14,128,32,128]{3,2,1,0:T(8,128)(2,1)S(1)} %bitcast.104) | data formatting | bytes 29360128 | tf_op jit(solution)/shard_map/reshape | solution.py:33
  254.2 0.0 copy-done.2
  254.2 1.9 copy.27
  256.1 13.7 %scatter_fusion = bf16[14,128,32,128]{3,1,2,0:T(8,128)(2,1)} fusion(bf16[14,128,32,128]{3,1,2,0:T(8,128)(2,1)} %copy.22, s32[64]{0:T(128)S(1)} %get-tuple-element.27, bf16[64,128,128]{2,1,0:T(8,128)(2,1)} %bitcast.108), kind=kCustom, calls=%fused_computation.4 | custom fusion | flops 1048576 | bytes 6291968 | tf_op jit(solution)/shard_map/scatter-add | solution.py:34
  269.8 0.0 copy-start.5
  269.8 13.1 %copy.23 = bf16[14,128,32,128]{3,2,1,0:T(8,128)(2,1)S(1)} copy(bf16[14,128,32,128]{3,1,2,0:T(8,128)(2,1)} %scatter_fusion) | data formatting | bytes 29360128 | tf_op jit(solution)/shard_map/scatter-add | solution.py:34
  282.9 0.0 copy-done.5
  282.9 15.6 %fusion.6 = bf16[512,1792]{0,1:T(8,128)(2,1)} fusion(bf16[512,4096]{1,0:T(8,128)(2,1)} %all-gather.3.cloned.1.call-done, bf16[224,8,32,128]{3,2,1,0:T(8,128)(2,1)S(1)} %bitcast.107), kind=kOutput, calls=%fused_computation.12 | convolution fusion | flops 7517110272 | bytes 20709376 | tf_op jit(solution)/shard_map/dot_general | solution.py:36
  298.6 3.8 %copy.25 = bf16[512,1792]{1,0:T(8,128)(2,1)} copy(bf16[512,1792]{0,1:T(8,128)(2,1)} %fusion.6) | data formatting | bytes 3670016
  302.3 2.1 fusion.12
  304.5 0.0 all-gather.5.cloned.1.call-done
  304.5 7.9 %gather_fusion.3 = bf16[64,16384]{1,0:T(8,128)(2,1)} fusion(bf16[128,16384]{1,0:T(8,128)(2,1)} %all-gather.5.cloned.1.call-done, s32[1024]{0:T(1024)S(1)} %pad_clamp_fusion), kind=kCustom, calls=%fused_computation.3 | custom fusion | bytes 4194560 | tf_op jit(solution)/shard_map/jit(_take)/gather | solution.py:79
  312.4 3.2 broadcast_select_fusion
  315.5 0.0 copy-done.1
  (9 shorter events, 0.1 us)
Async XLA Ops:
  7.2 37.4 %copy-start = (bf16[512,1792]{1,0:T(8,128)(2,1)S(1)}, bf16[512,1792]{1,0:T(8,128)(2,1)}, u32[]{:S(2)}) copy-start(bf16[512,1792]{1,0:T(8,128)(2,1)} %param.8) | copy-start | bytes 5505028
  7.2 37.4 %all-gather.3.cloned.1.call-start = ((), (), s32[]{:S(2)}) async-start(), calls=%async_computation | async-start | bytes 4718592 | tf_op jit(solution)/shard_map/all_gather | solution.py:29
  7.9 226.9 %all-reduce.3.cloned.1.call-start = ((), (), s32[]{:S(2)}) async-start(), calls=%async_computation.2 | async-start | bytes 8388608
  131.5 3.1 copy-start.6
  131.5 103.3 %copy-start.3 = (f32[1,8,16384]{2,1,0:T(8,128)S(1)}, f32[1,8,16384]{2,1,0:T(8,128)}, u32[]{:S(2)}) copy-start(f32[1,8,16384]{2,1,0:T(8,128)} %param.15) | copy-start | bytes 1572868
  131.5 103.3 %copy-start.4 = (f32[1,8,16384]{2,1,0:T(8,128)S(1)}, f32[1,8,16384]{2,1,0:T(8,128)}, u32[]{:S(2)}) copy-start(f32[1,8,16384]{2,1,0:T(8,128)} %param.14) | copy-start | bytes 1572868
  131.6 172.9 %all-gather.5.cloned.1.call-start = ((), (), s32[]{:S(2)}) async-start(), calls=%async_computation.1 | async-start | bytes 4456448 | tf_op jit(solution)/shard_map/all_gather | solution.py:78
  245.9 8.3 %copy-start.2 = (bf16[64,16384]{1,0:T(8,128)(2,1)S(1)}, bf16[64,16384]{1,0:T(8,128)(2,1)}, u32[]{:S(2)}) copy-start(bf16[64,16384]{1,0:T(8,128)(2,1)} %param.11) | copy-start | bytes 6291460
  269.8 13.1 %copy-start.5 = (s32[64,1]{0,1:T(1,128)S(1)}, s32[64,1]{0,1:T(1,128)}, u32[]{:S(2)}) copy-start(s32[64,1]{0,1:T(1,128)} %param.13) | copy-start | bytes 772
  304.5 11.0 %copy-start.1 = (bf16[512,1792]{1,0:T(8,128)(2,1)S(1)}, bf16[512,1792]{1,0:T(8,128)(2,1)}, u32[]{:S(2)}) copy-start(bf16[512,1792]{1,0:T(8,128)(2,1)} %param.8) | copy-start | bytes 5505028
Sparse Core Ops, SparseCore 0:
  9.7 34.7 all-gather.2
  131.7 103.0 all-reduce.2
  237.1 51.1 all-gather.4
where the time goes:
time: 324 us; the launch traced here: 322 us
  waiting for transfers between devices  134 us (41%)
  local copies, waits for them, and re-layouts  112 us (35%)
  matrix products  31.4 us (10%)
  other arithmetic  29.9 us (9%)
  between operations  14.5 us (4%)
    unnamed x4, waiting for transfers between devices  99.6 us
    unnamed x20, local copies, waits for them, and re-layouts  37.1 us
    all_gather x1, waiting for transfers between devices, local(): full_dy = lax.all_gather(cotangent, 'mp', axis=1, tiled=True)  34.1 us
    reshape x1, local copies, waits for them, and re-layouts, local(): product_view = products.reshape(row_blocks, BS, col_blocks, BS)  19.1 us
    dot_general x1, matrix products, local(): lax.dot_general(hidden_act, full_dy, outer_dims, preferred_element_type=j...  15.8 us
    dot_general x1, matrix products, local(): lax.dot_general(full_dy, merged, dims, preferred_element_type=jnp.float32)  15.6 us
    scatter-add x1, other arithmetic, local(): weight_view.at[block_rows, :, block_cols, :].add(delta_tiles)  13.7 us
    scatter-add x1, local copies, waits for them, and re-layouts, local(): weight_view.at[block_rows, :, block_cols, :].add(delta_tiles)  13.1 us
  transfers between devices with their start and end apart: 3, of which 2 were waited for; matrix products, arithmetic and copies ran while one was open for 23% of the time, Pallas kernels for 0%

commit v1 on v0

v1 whole, which is shorter than its diff:
```python
import functools
import math

import jax
import jax.numpy as jnp
from jax import lax
from jax.experimental import pallas as pl
from jax.experimental.pallas import tpu as pltpu
from jax.sharding import PartitionSpec as P

D = 4096
BS = 128
TOK = 512
FFL = 1792
RB = 14
CB = 32
NBL = 64
CAP = 8
TILES = 7
TILE = FFL // TILES

BETA_ONE = 0.9
BETA_TWO = 0.95
LEARN_RATE = 0.02
EPSILON = 1e-08
CORRECT_ONE = 1.0 - 0.9**4
CORRECT_TWO = 1.0 - 0.95**4
GRAD_SCALE = 1.0 / math.sqrt(8192.0)

MESH = pl.DeviceIdType.MESH
BF16, F32, I32 = jnp.bfloat16, jnp.float32, jnp.int32
N_REMOTE = 64


def mod4(v):
    return lax.rem(v + 4, 4)


def kernel(
    cot, hid, weight, deltas, dblocks, ids_row, own_row, first, second,
    grad_out, deltas_out, first_out, second_out,
    cbuf, hbuf, ht, dense, wbuf, drow, dblk, stage, rx, ry, cb, r1, rx2, ry2, cb2, gsum,
    gath, mbuf, vbuf, mnew, vnew, cur, dnew, obuf, tab, stab, pick,
    lsem, wsem, osem, ssem, rsem,
):
    dp, mp = lax.axis_index("dp"), lax.axis_index("mp")
    xx, yy = dp // 4, lax.rem(dp, 4)
    zz, core = mp // 2, lax.rem(mp, 2)
    x_up, x_dn = (mod4(xx + 1) * 4 + yy, mp), (mod4(xx - 1) * 4 + yy, mp)
    y_up, y_dn = (xx * 4 + mod4(yy + 1), mp), (xx * 4 + mod4(yy - 1), mp)
    z_up, z_dn = (dp, mod4(zz + 1) * 2 + core), (dp, mod4(zz - 1) * 2 + core)
    mate = (dp, zz * 2 + 1 - core)

    def local_copy(src, dst, i):
        c = pltpu.make_async_copy(src, dst, lsem.at[i])
        c.start()
        return c

    def col(z, c, half, width=256):
        return pl.ds(pl.multiple_of((z * 2 + c) * 512 + half * 256, 256), width)

    cp_cot = local_copy(cot, cbuf.at[:, col(zz, core, 0, 512)], 0)
    cp_hid = local_copy(hid, hbuf, 1)
    cp_dr = local_copy(deltas, drow, 2)
    cp_m = local_copy(first, mbuf, 3)
    cp_v = local_copy(second, vbuf, 4)
    cp_db = local_copy(dblocks, dblk.at[pl.ds(0, NBL)], 5)

    def w_copy(n, slot):
        return pltpu.make_async_copy(
            weight.at[pl.ds(pl.multiple_of(n * TILE, TILE), TILE)], wbuf.at[slot], wsem.at[slot])

    w_copy(0, 0).start()

    barrier = pltpu.get_barrier_semaphore()
    for dev in (x_up, x_dn, y_up, y_dn, z_up, z_dn, mate):
        pl.semaphore_signal(barrier, inc=1, device_id=dev, device_id_type=MESH)
    pl.semaphore_wait(barrier, 7)

    sent = []

    def send(src, dst, dev):
        i = len(sent)
        c = pltpu.make_async_remote_copy(
            src_ref=src, dst_ref=dst, send_sem=ssem.at[i], recv_sem=rsem.at[i],
            device_id=dev, device_id_type=MESH)
        c.start()
        sent.append(c)
        return c

    def share(where, dev):
        return send(cbuf.at[:, where], cbuf.at[:, where], dev)

    cp_cot.wait()
    up_a = share(col(zz, core, 0), z_up)
    dn_b = share(col(zz, core, 1), z_dn)
    to_mate = share(col(zz, core, 0, 512), mate)
    up_b = share(col(zz, core, 1), z_up)
    dn_a = share(col(zz, core, 0), z_dn)

    ri = lax.broadcasted_iota(I32, (NBL, NBL), 0)
    ci = lax.broadcasted_iota(I32, (NBL, NBL), 1)
    eye = ri == ci
    owns = jnp.broadcast_to(own_row[...], (NBL, NBL))
    own_col = jnp.sum(jnp.where(eye, owns, 0), axis=1, keepdims=True)
    ids_col = jnp.sum(jnp.where(eye, jnp.broadcast_to(ids_row[...], (NBL, NBL)), 0), axis=1, keepdims=True)
    slot_col = jnp.sum(jnp.where((own_col == owns) & (ci < ri), 1, 0), axis=1, keepdims=True)
    target_col = own_col * CAP + slot_col
    target_row = jnp.sum(jnp.where(eye, jnp.broadcast_to(target_col, (NBL, NBL)), 0), axis=0, keepdims=True)
    block_at = lax.broadcasted_iota(I32, (NBL, 512), 1)
    number = lax.broadcasted_iota(I32, (NBL, 512), 0)
    inverse = NBL - jnp.max(jnp.where(ids_col == block_at, NBL - number, 0), axis=0, keepdims=True)
    place = jnp.max(jnp.where(target_col == block_at, jnp.broadcast_to(ids_col, (NBL, 512)), 0), axis=0, keepdims=True)
    tab[...] = jnp.zeros_like(tab)
    tab[0:1, :] = inverse
    tab[1:2, :] = place
    cp_tab = local_copy(tab, stab, 6)
    mine = lax.broadcasted_iota(I32, (16, NBL), 0)
    hit = jnp.where((target_row == dp * CAP + mine) & (mine < CAP), 1.0, 0.0)
    filled = jnp.sum(hit, axis=1, keepdims=True)[0:CAP] > 0.5
    q = lax.broadcasted_iota(I32, (NBL, 256), 1)
    for h in range(2):
        dev_at = own_col if h else lax.rem(own_col, 4) * 4 + own_col // 4
        for half in range(2):
            pick[h, half] = jnp.where(q == dev_at * 16 + half * 8 + slot_col, 1.0, 0.0).astype(BF16)

    cp_hid.wait()

    @pl.loop(0, TILES)
    def _(i):
        rows = pl.ds(pl.multiple_of(i * TILE, TILE), TILE)
        ht[rows, :] = hbuf[:, rows].T

    def products(z, c, half, width):
        first_col = (z * 2 + c) * 4 + half * 2
        where = col(z, c, half, width)

        @pl.loop(0, TILES)
        def _(i):
            rows = pl.ds(pl.multiple_of(i * TILE, TILE), TILE)
            g = jnp.dot(ht[rows, :], cbuf[:, where], preferred_element_type=F32).astype(BF16)
            for r in range(2):
                for k in range(width // BS):
                    dense[(i * 2 + r) * CB + first_col + k] = g[r * BS:(r + 1) * BS, k * BS:(k + 1) * BS]

    mate_core = 1 - core
    zu, zd, zo = mod4(zz + 1), mod4(zz - 1), mod4(zz + 2)
    products(zz, core, 0, 512)
    to_mate.wait_recv()
    products(zz, mate_core, 0, 512)
    up_a.wait_recv()
    fw_a = share(col(zd, core, 0), z_up)
    m_da = share(col(zd, core, 0), mate)
    dn_b.wait_recv()
    fw_b = share(col(zu, core, 1), z_dn)
    m_ub = share(col(zu, core, 1), mate)
    products(zd, core, 0, 256)
    products(zu, core, 1, 256)
    m_da.wait_recv()
    products(zd, mate_core, 0, 256)
    m_ub.wait_recv()
    products(zu, mate_core, 1, 256)
    up_b.wait_recv()
    m_db = share(col(zd, core, 1), mate)
    dn_a.wait_recv()
    m_ua = share(col(zu, core, 0), mate)
    products(zd, core, 1, 256)
    products(zu, core, 0, 256)
    m_db.wait_recv()
    products(zd, mate_core, 1, 256)
    m_ua.wait_recv()
    products(zu, mate_core, 0, 256)
    fw_a.wait_recv()
    m_oa = share(col(zo, core, 0), mate)
    fw_b.wait_recv()
    m_ob = share(col(zo, core, 1), mate)
    products(zo, core, 0, 512)
    m_oa.wait_recv()
    m_ob.wait_recv()
    products(zo, mate_core, 0, 512)

    cp_tab.wait()
    cp_db.wait()
    dblk[NBL] = jnp.zeros((BS, BS), BF16)

    def out_copy(n, slot):
        return pltpu.make_async_copy(
            obuf.at[slot], grad_out.at[:, pl.ds(pl.multiple_of(n * TILE, TILE), TILE)], osem.at[slot])

    def tile(n):
        slot = n % 2
        if n + 1 < TILES:
            w_copy(n + 1, 1 - slot).start()
        w_copy(n, slot).wait()

        @pl.loop(0, CB)
        def _(c):
            for r in range(2):
                k = stab[0, (n * 2 + r) * CB + c]
                cols = pl.ds(pl.multiple_of(c * BS, BS), BS)
                wbuf[slot, r * BS:(r + 1) * BS, cols] += dblk[k]

        if n >= 2:
            out_copy(n - 2, slot).wait()

        @pl.loop(0, 2)
        def _(m):
            rows = pl.ds(pl.multiple_of(m * 256, 256), 256)
            obuf[slot, rows, :] = lax.dot_general(
                cbuf[rows, :], wbuf[slot], (((1,), (1,)), ((), ())), preferred_element_type=F32).astype(BF16)

        out_copy(n, slot).start()

    axes = ((xx, x_up, x_dn), (yy, y_up, y_dn))
    us = [(axes[h][0], axes[h][1], axes[h][2]) for h in range(2)]
    ws = [(axes[1 - h][0], axes[1 - h][1], axes[1 - h][2]) for h in range(2)]

    def fill(h, quarter, ab):
        @pl.loop(0, 8)
        def _(j):
            o, i = j // 2, lax.rem(j, 2)
            dev = o * 4 + quarter if h else quarter * 4 + o
            t = dev * CAP + h * 4 + ab * 2 + i
            stage[h, quarter, ab, o, i] = dense[stab[1, t]]

    s1 = [None, None]
    for h in range(2):
        u, up, dn = us[h]
        opp = mod4(u + 2)
        fill(h, opp, 0)
        a1 = send(stage.at[h, opp, 0], rx.at[h, 0], up)
        fill(h, opp, 1)
        b1 = send(stage.at[h, opp, 1], rx.at[h, 1], dn)
        s1[h] = [a1, b1]
    for h in range(2):
        u, up, dn = us[h]
        qu, qd = mod4(u + 1), mod4(u - 1)
        fill(h, qu, 1)
        a2 = send(stage.at[h, qu, 1], ry.at[h, 0, 1], up)
        fill(h, qd, 0)
        b2 = send(stage.at[h, qd, 0], ry.at[h, 1, 0], dn)
        s1[h] += [a2, b2]
    for h in range(2):
        u, up, dn = us[h]
        fill(h, mod4(u + 1), 0)
        fill(h, mod4(u - 1), 1)
        fill(h, u, 0)
        fill(h, u, 1)

    def add2(dst, a, b):
        @pl.loop(0, 4)
        def _(o):
            dst[o] = (a[o].astype(F32) + b[o].astype(F32)).astype(BF16)

    tile(0)
    tile(1)
    for h in range(2):
        u, up, dn = us[h]
        a1, b1, a2, b2 = s1[h]
        a1.wait_recv()
        add2(cb.at[h, 0], stage.at[h, mod4(u + 1), 0], rx.at[h, 0])
        a3 = send(cb.at[h, 0], ry.at[h, 0, 0], up)
        b1.wait_recv()
        add2(cb.at[h, 1], stage.at[h, mod4(u - 1), 1], rx.at[h, 1])
        b3 = send(cb.at[h, 1], ry.at[h, 1, 1], dn)
        s1[h] += [a3, b3]
    tile(2)
    tile(3)
    s2 = [None, None]
    for h in range(2):
        u, up, dn = us[h]
        w, wup, wdn = ws[h]
        a1, b1, a2, b2, a3, b3 = s1[h]
        for ab, pair in ((0, (a3, b2)), (1, (a2, b3))):
            for c in pair:
                c.wait_recv()

            @pl.loop(0, 4)
            def _(o):
                r1[h, ab, o] = (
                    stage[h, u, ab, o].astype(F32) + ry[h, 0, ab, o].astype(F32) + ry[h, 1, ab, o].astype(F32)
                ).astype(BF16)
        wopp, wqu, wqd = mod4(w + 2), mod4(w + 1), mod4(w - 1)
        s2[h] = [
            send(r1.at[h, 0, wopp], rx2.at[h, 0], wup),
            send(r1.at[h, 1, wopp], rx2.at[h, 1], wdn),
            send(r1.at[h, 1, wqu], ry2.at[h, 0, 1], wup),
            send(r1.at[h, 0, wqd], ry2.at[h, 1, 0], wdn),
        ]
    tile(4)
    for h in range(2):
        w, wup, wdn = ws[h]
        a1, b1, a2, b2 = s2[h]
        a1.wait_recv()
        cb2[h, 0] = (r1[h, 0, mod4(w + 1)].astype(F32) + rx2[h, 0].astype(F32)).astype(BF16)
        a3 = send(cb2.at[h, 0], ry2.at[h, 0, 0], wup)
        b1.wait_recv()
        cb2[h, 1] = (r1[h, 1, mod4(w - 1)].astype(F32) + rx2[h, 1].astype(F32)).astype(BF16)
        b3 = send(cb2.at[h, 1], ry2.at[h, 1, 1], wdn)
        s2[h] += [a3, b3]
    cp_dr.wait()
    hit16 = hit.astype(BF16)

    @pl.loop(0, 32)
    def _(i):
        lanes = pl.ds(pl.multiple_of(i * 512, 512), 512)
        cur[:, lanes] = jnp.dot(hit16, drow[:, lanes], preferred_element_type=F32)

    for h in range(2):
        w, wup, wdn = ws[h]
        a1, b1, a2, b2, a3, b3 = s2[h]
        for ab, pair in ((0, (a3, b2)), (1, (a2, b3))):
            for c in pair:
                c.wait_recv()
            for i in range(2):
                gsum[pl.ds((h * 4 + ab * 2 + i) * BS, BS), :] = (
                    r1[h, ab, w, i].astype(F32) + ry2[h, 0, ab, i].astype(F32) + ry2[h, 1, ab, i].astype(F32))
    cp_m.wait()
    cp_v.wait()

    def adam(r):
        lanes = pl.ds(pl.multiple_of(r * BS, BS), BS)
        g = gsum[pl.ds(r, CAP, stride=BS), :] * GRAD_SCALE
        m0, v0 = mbuf[:, lanes], vbuf[:, lanes]
        m1 = BETA_ONE * m0 + (1.0 - BETA_ONE) * g
        v1 = BETA_TWO * v0 + (1.0 - BETA_TWO) * g * g
        stepped = cur[0:CAP, lanes] - LEARN_RATE * (m1 / CORRECT_ONE) / (jnp.sqrt(v1 / CORRECT_TWO) + EPSILON)
        mnew[:, lanes] = jnp.where(filled, m1, m0)
        vnew[:, lanes] = jnp.where(filled, v1, v0)
        return jnp.where(filled, stepped, 0.0)

    g1 = [[], []]
    for h in range(2):
        group, member = (yy, xx) if h == 0 else (xx, yy)
        u, up, dn = us[h]
        for ab in range(2):
            @pl.loop(0, 16)
            def _(j):
                r = h * 32 + ab * 16 + j
                both = jnp.concatenate([adam(r), adam(r + 64)], axis=0).astype(BF16)
                gath[h, group, ab, member, :, pl.ds(pl.multiple_of(j * BS, BS), BS)] = both
            own = gath.at[h, group, ab, member]
            g1[h] += [send(own, own, up), send(own, own, dn)]
    out_m = local_copy(mnew, first_out, 7)
    out_v = local_copy(vnew, second_out, 8)
    tile(5)
    for h in range(2):
        group, member = (yy, xx) if h == 0 else (xx, yy)
        u, up, dn = us[h]
        up0, dn0, up1, dn1 = g1[h]
        up0.wait_recv()
        piece = gath.at[h, group, 0, mod4(member - 1)]
        f_up = send(piece, piece, up)
        dn1.wait_recv()
        piece = gath.at[h, group, 1, mod4(member + 1)]
        f_dn = send(piece, piece, dn)
        g1[h] += [f_up, f_dn]
    g2 = [[], []]
    for h in range(2):
        group = yy if h == 0 else xx
        w, wup, wdn = ws[h]
        up0, dn0, up1, dn1, f_up, f_dn = g1[h]
        dn0.wait_recv()
        f_up.wait_recv()
        piece = gath.at[h, group, 0]
        g2[h] += [send(piece, piece, wup), send(piece, piece, wdn)]
        up1.wait_recv()
        f_dn.wait_recv()
        piece = gath.at[h, group, 1]
        g2[h] += [send(piece, piece, wup), send(piece, piece, wdn)]
    tile(6)
    for h in range(2):
        group = yy if h == 0 else xx
        w, wup, wdn = ws[h]
        up0, dn0, up1, dn1 = g2[h]
        up0.wait_recv()
        piece = gath.at[h, mod4(group - 1), 0]
        f_up = send(piece, piece, wup)
        dn1.wait_recv()
        piece = gath.at[h, mod4(group + 1), 1]
        f_dn = send(piece, piece, wdn)
        g2[h] += [f_up, f_dn]

    for ab in range(2):
        for h in range(2):
            up0, dn0, up1, dn1, f_up, f_dn = g2[h]
            for c in ((dn0, f_up), (up1, f_dn))[ab]:
                c.wait_recv()

            @pl.loop(0, 4)
            def _(i):
                x = gath[h, :, ab, :, :, pl.ds(pl.multiple_of(i * 512, 512), 512)].reshape(256, 512)
                for half in range(2):
                    lanes = pl.ds(pl.multiple_of(half * 8192 + h * 4096 + ab * 2048 + i * 512, 512), 512)
                    dnew[:, lanes] = jnp.dot(pick[h, half], x, preferred_element_type=F32).astype(BF16)
    out_d = local_copy(dnew, deltas_out, 9)
    for c in sent:
        c.wait_send()
    out_m.wait()
    out_v.wait()
    out_copy(TILES - 2, (TILES - 2) % 2).wait()
    out_copy(TILES - 1, (TILES - 1) % 2).wait()
    out_d.wait()


def local(hidden_act, cotangent, weight, deltas, block_ids, owners, first_moment, second_moment):
    any_spec = pl.BlockSpec(memory_space=pl.ANY)
    vm_spec = pl.BlockSpec(memory_space=pltpu.VMEM)
    V = pltpu.VMEM
    outs = pl.pallas_call(
        kernel,
        out_shape=(
            jax.ShapeDtypeStruct((TOK, FFL), BF16),
            jax.ShapeDtypeStruct((NBL, BS * BS), BF16),
            jax.ShapeDtypeStruct((CAP, BS * BS), F32),
            jax.ShapeDtypeStruct((CAP, BS * BS), F32),
        ),
        in_specs=[any_spec] * 5 + [vm_spec] * 2 + [any_spec] * 2,
        out_specs=(any_spec,) * 4,
        scratch_shapes=[
            V((TOK, D), BF16),
            V((TOK, FFL), BF16),
            V((FFL, TOK), BF16),
            V((RB * CB, BS, BS), BF16),
            V((2, TILE, D), BF16),
            V((NBL, BS * BS), BF16),
            V((NBL + 1, BS, BS), BF16),
            V((2, 4, 2, 4, 2, BS, BS), BF16),
            V((2, 2, 4, 2, BS, BS), BF16),
            V((2, 2, 2, 4, 2, BS, BS), BF16),
            V((2, 2, 4, 2, BS, BS), BF16),
            V((2, 2, 4, 2, BS, BS), BF16),
            V((2, 2, 2, BS, BS), BF16),
            V((2, 2, 2, 2, BS, BS), BF16),
            V((2, 2, 2, BS, BS), BF16),
            V((CAP * BS, BS), F32),
            V((2, 4, 2, 4, 16, 2048), BF16),
            V((CAP, BS * BS), F32),
            V((CAP, BS * BS), F32),
            V((CAP, BS * BS), F32),
            V((CAP, BS * BS), F32),
            V((16, BS * BS), F32),
            V((NBL, BS * BS), BF16),
            V((2, TOK, TILE), BF16),
            V((8, 512), I32),
            pltpu.SMEM((8, 512), I32),
            V((2, 2, NBL, 256), BF16),
            pltpu.SemaphoreType.DMA((10,)),
            pltpu.SemaphoreType.DMA((2,)),
            pltpu.SemaphoreType.DMA((2,)),
            pltpu.SemaphoreType.DMA((N_REMOTE,)),
            pltpu.SemaphoreType.DMA((N_REMOTE,)),
        ],
        compiler_params=pltpu.CompilerParams(
            collective_id=0, has_side_effects=True, vmem_limit_bytes=60 * 1024 * 1024),
        cost_estimate=pl.CostEstimate(flops=15 * 10**9, bytes_accessed=25 * 10**6, transcendentals=0),
    )(
        cotangent, hidden_act, weight, deltas, deltas.reshape(NBL, BS, BS),
        block_ids.reshape(1, NBL), owners.reshape(1, NBL), first_moment[0], second_moment[0],
    )
    input_grad, new_deltas, new_first, new_second = outs
    return (input_grad, new_deltas, new_first[None], new_second[None])


def solution(mesh):
    in_specs = (
        P("dp", "mp"),
        P("dp", "mp"),
        P("mp", None),
        P("mp", None),
        P("mp"),
        P("mp", None),
        P("mp", "dp", None),
        P("mp", "dp", None),
    )
    out_specs = (P("dp", "mp"), P("mp", None), P("mp", "dp", None), P("mp", "dp", None))
    return jax.shard_map(local, mesh=mesh, in_specs=in_specs, out_specs=out_specs, check_vma=False)
```

time: 324 us -> 103 us (0.32)
  waiting for transfers between devices: 134 us -> 0 us
  local copies, waits for them, and re-layouts: 112 us -> 9.45 us
  Pallas kernels: 0 us -> 93.2 us
  matrix products: 31.4 us -> 0 us
  other arithmetic: 29.9 us -> 0 us
  between operations: 14.5 us -> 0.65 us
    unnamed x4 -> x0, waiting for transfers between devices: 99.6 us -> none
    pallas_call x0 -> x1, Pallas kernels: none -> 93.2 us  [local(): pl.pallas_call(kernel, out_shape=(jax.ShapeDtypeStruct((TOK, FFL), BF16),...]
    gather x4 -> x0, local copies, waits for them, and re-layouts: 34.8 us -> none  [the longest x1 12.2 us: local(): product_view[block_rows, :, block_cols, :].reshape(count_blocks, BS * BS)]
    all_gather x2 -> x0, waiting for transfers between devices: 34.1 us -> none  [the longest x1 34.1 us: local(): full_dy = lax.all_gather(cotangent, 'mp', axis=1, tiled=True)]
    dot_general x2 -> x0, matrix products: 31.4 us -> none  [the longest x1 15.8 us: local(): lax.dot_general(hidden_act, full_dy, outer_dims, preferred_element_type=j...]
    unnamed x20 -> x11, local copies, waits for them, and re-layouts: 37.1 us -> 9.45 us
    reshape x2 -> x0, local copies, waits for them, and re-layouts: 27.4 us -> none  [the longest x1 19.1 us: local(): product_view = products.reshape(row_blocks, BS, col_blocks, BS)]
    scatter-add x1 -> x0, other arithmetic: 13.7 us -> none  [local(): weight_view.at[block_rows, :, block_cols, :].add(delta_tiles)]
  transfers between devices with their start and end apart: 3 -> 0, of which waited for: 2 -> 0; matrix products, arithmetic and copies ran while one was open for 23% -> 0% of each run, Pallas kernels for 0% -> 0%
where the time goes in v1:
time: 103 us
  Pallas kernels  93.2 us (90%)
  local copies, waits for them, and re-layouts  9.45 us (9%)
    pallas_call x1, Pallas kernels, local(): pl.pallas_call(kernel, out_shape=(jax.ShapeDtypeStruct((TOK, FFL), BF16),...  93.2 us
    unnamed x11, local copies, waits for them, and re-layouts  9.45 us

profile of v1, /device:TPU:0, one launch (start us, length us, event | category | flops | bytes accessed | tf_op | source)
XLA Modules:
  0.0 103.3 jit_solution(14797725974687697864)
XLA Ops:
  0.6 3.5 %copy.12 = bf16[8,8,128,128]{3,2,1,0:T(8,128)(2,1)} copy(bf16[8,8,128,128]{3,1,2,0:T(8,128)(2,1)} %bitcast.8) | data formatting | bytes 4194304
  4.1 93.2 %shard_map.111 = (bf16[512,1792]{1,0:T(8,128)(2,1)}, bf16[64,16384]{1,0:T(8,128)(2,1)}, f32[8,16384]{1,0:T(8,128)}, f32[8,16384]{1,0:T(8,128)}) custom-call(bf16[512,512]{1,0:T(8,128)(2,1)} %cot.1, bf16[512,1792]{1,0:T(8,128)(2,1)} %hid.1, bf16[1792,4096]{1,0:T(8,128)(2,1)} %weight.1, bf16[64,16384]{1,0:T(8,128)(2,1)} %deltas.1, ...), custom_call_target="tpu_custom_call" | custom-call | flops 15000000512 | bytes 25000000 | tf_op jit(solution)/shard_map/pallas_call | solution.py:410
  97.3 0.0 copy-start
  97.3 3.0 %copy.17 = bf16[512,1792]{1,0:T(8,128)(2,1)} copy(bf16[512,1792]{1,0:T(8,128)(2,1)} %get-tuple-element.16) | data formatting | bytes 3670016
  100.3 0.0 copy-done
  100.3 0.0 copy-start.2
  100.3 0.0 copy-start.1
  100.3 1.3 %copy.18 = bf16[64,16384]{1,0:T(8,128)(2,1)} copy(bf16[64,16384]{1,0:T(8,128)(2,1)S(1)} %copy-done) | data formatting | bytes 4194304
  101.6 0.1 copy-done.2
  101.7 0.8 copy.19
  102.5 0.0 copy-done.1
  102.5 0.8 copy.20
Async XLA Ops:
  97.3 3.0 %copy-start = (bf16[64,16384]{1,0:T(8,128)(2,1)S(1)}, bf16[64,16384]{1,0:T(8,128)(2,1)}, u32[]{:S(2)}) copy-start(bf16[64,16384]{1,0:T(8,128)(2,1)} %get-tuple-element.17) | copy-start | bytes 6291460
  100.3 1.4 %copy-start.2 = (f32[8,16384]{1,0:T(8,128)S(1)}, f32[8,16384]{1,0:T(8,128)}, u32[]{:S(2)}) copy-start(f32[8,16384]{1,0:T(8,128)} %get-tuple-element.10) | copy-start | bytes 1572868
  100.3 2.2 %copy-start.1 = (f32[8,16384]{1,0:T(8,128)S(1)}, f32[8,16384]{1,0:T(8,128)}, u32[]{:S(2)}) copy-start(f32[8,16384]{1,0:T(8,128)} %get-tuple-element.11) | copy-start | bytes 1572868

commit v2 on v1

v2 whole, which is shorter than its diff:
```python
import functools
import math

import jax
import jax.numpy as jnp
from jax import lax
from jax.experimental import pallas as pl
from jax.experimental.pallas import tpu as pltpu
from jax.sharding import PartitionSpec as P

D = 4096
BS = 128
TOK = 512
FFL = 1792
RB = 14
CB = 32
NBL = 64
CAP = 8
TILES = 7
TILE = FFL // TILES

BETA_ONE = 0.9
BETA_TWO = 0.95
LEARN_RATE = 0.02
EPSILON = 1e-08
CORRECT_ONE = 1.0 - 0.9**4
CORRECT_TWO = 1.0 - 0.95**4
GRAD_SCALE = 1.0 / math.sqrt(8192.0)

MESH = pl.DeviceIdType.MESH
BF16, F32, I32 = jnp.bfloat16, jnp.float32, jnp.int32
N_REMOTE = 80


def mod4(v):
    return lax.rem(v + 4, 4)


def kernel(
    cot, hid, weight, deltas, ids_row, own_row, first, second,
    grad_out, deltas_out, first_out, second_out,
    cbuf, hbuf, ht, dense, wbuf, drow, dblk, stage, rx, ry, cb, r1, ry2, gsum,
    agm, sbm, rbm, agg, sbg, rbg, gath, g16, cur, mbuf, vbuf, mnew, vnew, dnew, obuf, tab, stab,
    sel_m, sel_g, sel_d, lsem, wsem, osem, dsem, ssem, rsem,
):
    dp, mp = lax.axis_index("dp"), lax.axis_index("mp")
    xx, yy = dp // 4, lax.rem(dp, 4)
    zz, core = mp // 2, lax.rem(mp, 2)
    x_dev = [(mod4(xx + d) * 4 + yy, mp) for d in range(4)]
    y_dev = [(xx * 4 + mod4(yy + d), mp) for d in range(4)]
    z_up, z_dn = (dp, mod4(zz + 1) * 2 + core), (dp, mod4(zz - 1) * 2 + core)
    mate = (dp, zz * 2 + 1 - core)
    us = ((xx, x_dev), (yy, y_dev))
    ws = ((yy, y_dev), (xx, x_dev))

    def local_copy(src, dst, i):
        c = pltpu.make_async_copy(src, dst, lsem.at[i])
        c.start()
        return c

    def col(z, c, half, width=256):
        return pl.ds(pl.multiple_of((z * 2 + c) * 512 + half * 256, 256), width)

    cp_cot = local_copy(cot, cbuf.at[:, col(zz, core, 0, 512)], 0)
    cp_m = local_copy(first, mbuf, 3)
    cp_v = local_copy(second, vbuf, 4)
    cp_hid = local_copy(hid, hbuf, 1)
    cp_dr = local_copy(deltas, drow, 2)

    def w_copy(n, slot):
        return pltpu.make_async_copy(
            weight.at[pl.ds(pl.multiple_of(n * TILE, TILE), TILE)], wbuf.at[slot], wsem.at[slot])

    w_copy(0, 0).start()

    barrier = pltpu.get_barrier_semaphore()
    for dev in (*x_dev[1:], *y_dev[1:], z_up, z_dn, mate):
        pl.semaphore_signal(barrier, inc=1, device_id=dev, device_id_type=MESH)
    pl.semaphore_wait(barrier, 9)

    sent = []

    def send(src, dst, dev):
        i = len(sent)
        c = pltpu.make_async_remote_copy(
            src_ref=src, dst_ref=dst, send_sem=ssem.at[i], recv_sem=rsem.at[i],
            device_id=dev, device_id_type=MESH)
        c.start()
        sent.append(c)
        return c

    def share(where, dev):
        return send(cbuf.at[:, where], cbuf.at[:, where], dev)

    cp_cot.wait()
    up_a = share(col(zz, core, 0), z_up)
    dn_b = share(col(zz, core, 1), z_dn)
    to_mate = share(col(zz, core, 0, 512), mate)
    up_b = share(col(zz, core, 1), z_up)
    dn_a = share(col(zz, core, 0), z_dn)

    cp_m.wait()
    cp_v.wait()
    m1 = [None, None]
    for h in range(2):
        u, dev = us[h]
        for ab in range(2):
            @pl.loop(0, 8)
            def _(j):
                here = pl.ds(pl.multiple_of(j * 512, 512), 512)
                there = pl.ds(pl.multiple_of(h * 8192 + ab * 4096 + j * 512, 512), 512)
                agm[h, ab, u, :, here] = jnp.concatenate([mbuf[:, there], vbuf[:, there]], axis=0).astype(BF16)
        own = [agm.at[h, ab, u] for ab in range(2)]
        m1[h] = [send(own[0], own[0], dev[1]), send(own[1], own[1], dev[3]),
                 send(own[1], own[1], dev[1]), send(own[0], own[0], dev[3])]

    ri = lax.broadcasted_iota(I32, (NBL, NBL), 0)
    ci = lax.broadcasted_iota(I32, (NBL, NBL), 1)
    eye = ri == ci
    owns = jnp.broadcast_to(own_row[...], (NBL, NBL))
    own_col = jnp.sum(jnp.where(eye, owns, 0), axis=1, keepdims=True)
    ids_col = jnp.sum(jnp.where(eye, jnp.broadcast_to(ids_row[...], (NBL, NBL)), 0), axis=1, keepdims=True)
    slot_col = jnp.sum(jnp.where((own_col == owns) & (ci < ri), 1, 0), axis=1, keepdims=True)
    target_col = own_col * CAP + slot_col
    target_row = jnp.sum(jnp.where(eye, jnp.broadcast_to(target_col, (NBL, NBL)), 0), axis=0, keepdims=True)
    block_at = lax.broadcasted_iota(I32, (NBL, 512), 1)
    number = lax.broadcasted_iota(I32, (NBL, 512), 0)
    inverse = NBL - jnp.max(jnp.where(ids_col == block_at, NBL - number, 0), axis=0, keepdims=True)
    tab[...] = jnp.zeros_like(tab)
    tab[0:1, :] = inverse
    tab[1:2, 0:NBL] = ids_row[...]
    cp_tab = local_copy(tab, stab, 5)

    def one_hot(mask):
        return jnp.where(mask, 1.0, 0.0).astype(BF16)

    mine = lax.broadcasted_iota(I32, (16, NBL), 0)
    filled = jnp.max(jnp.where(target_row == dp * CAP + mine, 1, 0), axis=1, keepdims=True)[0:CAP] > 0
    for h in range(2):
        def dev_mem(v):
            return xx * 4 + v if h else v * 4 + yy

        def dev_dest(v):
            return v * 4 + yy if h else xx * 4 + v

        k = dev_dest(ri >> 4) * 4 + (ri & 3)
        wanted = jnp.sum(jnp.where(ci == k, jnp.broadcast_to(target_row, (NBL, NBL)), 0), axis=1, keepdims=True)
        hit = (wanted == dev_mem(ci >> 4) * CAP + (ci & 7)) & (((ri >> 3) & 1) == ((ci >> 3) & 1))
        for half in range(2):
            sel_m[h, half] = one_hot(hit & (((ri >> 2) & 1) == half))
        k = dev_mem(ci >> 4) * 4 + (ci & 3)
        goes = jnp.sum(jnp.where(ri == k, jnp.broadcast_to(target_col, (NBL, NBL)), 0), axis=0, keepdims=True)
        rg = lax.broadcasted_iota(I32, (128, NBL), 0)
        cg = lax.broadcasted_iota(I32, (128, NBL), 1)
        sel_g[h] = one_hot((goes == dev_dest(rg >> 5) * CAP + (rg & 7)) & (((rg >> 3) & 3) == ((cg >> 2) & 3)))
        rd = lax.broadcasted_iota(I32, (256, 256), 0)
        cd = lax.broadcasted_iota(I32, (256, 256), 1)
        group, mem = cd >> 6, (cd >> 4) & 3
        dev = group * 4 + mem if h else mem * 4 + group
        sel_d[h] = one_hot(((rd & 63) == dev * 4 + (cd & 3)) & ((rd >> 6) == ((cd >> 2) & 3)))

    cp_hid.wait()

    @pl.loop(0, TILES)
    def _(i):
        rows = pl.ds(pl.multiple_of(i * TILE, TILE), TILE)
        ht[rows, :] = hbuf[:, rows].T

    def products(z, c, half, width):
        first_col = (z * 2 + c) * 4 + half * 2
        where = col(z, c, half, width)

        @pl.loop(0, TILES)
        def _(i):
            rows = pl.ds(pl.multiple_of(i * TILE, TILE), TILE)
            g = jnp.dot(ht[rows, :], cbuf[:, where], preferred_element_type=F32).astype(BF16)
            for r in range(2):
                for k in range(width // BS):
                    dense[(i * 2 + r) * CB + first_col + k] = g[r * BS:(r + 1) * BS, k * BS:(k + 1) * BS]

    mate_core = 1 - core
    zu, zd, zo = mod4(zz + 1), mod4(zz - 1), mod4(zz + 2)
    products(zz, core, 0, 512)
    for h in range(2):
        u, dev = us[h]
        m1[h][0].wait_recv()
        piece = agm.at[h, 0, mod4(u - 1)]
        f_up = send(piece, piece, dev[1])
        m1[h][1].wait_recv()
        piece = agm.at[h, 1, mod4(u + 1)]
        f_dn = send(piece, piece, dev[3])
        m1[h] += [f_up, f_dn]
    to_mate.wait_recv()
    products(zz, mate_core, 0, 512)
    up_a.wait_recv()
    fw_a = share(col(zd, core, 0), z_up)
    m_da = share(col(zd, core, 0), mate)
    dn_b.wait_recv()
    fw_b = share(col(zu, core, 1), z_dn)
    m_ub = share(col(zu, core, 1), mate)
    products(zd, core, 0, 256)
    products(zu, core, 1, 256)
    m_da.wait_recv()
    products(zd, mate_core, 0, 256)
    m_ub.wait_recv()
    products(zu, mate_core, 1, 256)

    m2 = [None, None]
    for h in range(2):
        for c in m1[h][2:]:
            c.wait_recv()

        @pl.loop(0, 8)
        def _(j):
            here = pl.ds(pl.multiple_of(j * 512, 512), 512)
            both = 0.0
            for ab in range(2):
                x = agm[h, ab, :, :, here].reshape(64, 512)
                both = both + jnp.dot(sel_m[h, ab], x, preferred_element_type=F32)
            sbm[h, :, :, here] = both.astype(BF16).reshape(4, 16, 512)
        w, dev = ws[h]
        m2[h] = [send(sbm.at[h, mod4(w + d)], rbm.at[h, d], dev[d]) for d in (1, 3, 2)]

    up_b.wait_recv()
    m_db = share(col(zd, core, 1), mate)
    dn_a.wait_recv()
    m_ua = share(col(zu, core, 0), mate)
    products(zd, core, 1, 256)
    products(zu, core, 0, 256)
    m_db.wait_recv()
    products(zd, mate_core, 1, 256)
    m_ua.wait_recv()
    products(zu, mate_core, 0, 256)

    cp_dr.wait()
    rc = lax.broadcasted_iota(I32, (16, NBL), 0)
    cc = lax.broadcasted_iota(I32, (16, NBL), 1)
    my_row = cc == dp * 4 + (rc & 3)

    @pl.loop(0, 8)
    def _(j):
        here = pl.ds(pl.multiple_of(j * 512, 512), 512)
        rows = 0.0
        for quarter in range(4):
            there = pl.ds(pl.multiple_of(quarter * 4096 + j * 512, 512), 512)
            pick = one_hot(my_row & ((rc >> 2) == quarter))
            rows = rows + jnp.dot(pick, drow[:, there], preferred_element_type=F32)
        cur[:, here] = rows

    by_row = dblk.reshape((NBL + 1) * BS, BS)

    @pl.loop(0, BS)
    def _(r):
        by_row[pl.ds(r, NBL, stride=BS), :] = drow[:, pl.ds(pl.multiple_of(r * BS, BS), BS)].astype(F32)

    dblk[NBL] = jnp.zeros((BS, BS), F32)

    fw_a.wait_recv()
    m_oa = share(col(zo, core, 0), mate)
    fw_b.wait_recv()
    m_ob = share(col(zo, core, 1), mate)
    products(zo, core, 0, 512)
    m_oa.wait_recv()
    m_ob.wait_recv()
    products(zo, mate_core, 0, 512)
    cp_tab.wait()

    def out_copy(n, slot):
        return pltpu.make_async_copy(
            obuf.at[slot], grad_out.at[:, pl.ds(pl.multiple_of(n * TILE, TILE), TILE)], osem.at[slot])

    def tile(n):
        slot = n % 2
        if n + 1 < TILES:
            w_copy(n + 1, 1 - slot).start()
        w_copy(n, slot).wait()

        @pl.loop(0, CB)
        def _(c):
            for r in range(2):
                k = stab[0, (n * 2 + r) * CB + c]
                cols = pl.ds(pl.multiple_of(c * BS, BS), BS)
                add = dblk[k]
                old = wbuf[slot, r * BS:(r + 1) * BS, cols]
                wbuf[slot, r * BS:(r + 1) * BS, cols] = (old.astype(F32) + add).astype(BF16)

        if n >= 2:
            out_copy(n - 2, slot).wait()

        @pl.loop(0, 2)
        def _(m):
            rows = pl.ds(pl.multiple_of(m * 256, 256), 256)
            obuf[slot, rows, :] = lax.dot_general(
                cbuf[rows, :], wbuf[slot], (((1,), (1,)), ((), ())), preferred_element_type=F32).astype(BF16)

        out_copy(n, slot).start()

    def fill(h, quarter, ab):
        @pl.loop(0, 4)
        def _(o):
            dev = o * 4 + quarter if h else quarter * 4 + o
            stage[h, quarter, ab, o] = dense[stab[1, dev * 4 + h * 2 + ab]]

    s1 = [None, None]
    for h in range(2):
        u, dev = us[h]
        opp = mod4(u + 2)
        fill(h, opp, 0)
        a1 = send(stage.at[h, opp, 0], rx.at[h, 0], dev[1])
        fill(h, opp, 1)
        b1 = send(stage.at[h, opp, 1], rx.at[h, 1], dev[3])
        s1[h] = [a1, b1]
    for h in range(2):
        u, dev = us[h]
        qu, qd = mod4(u + 1), mod4(u - 1)
        fill(h, qu, 1)
        a2 = send(stage.at[h, qu, 1], ry.at[h, 0, 1], dev[1])
        fill(h, qd, 0)
        b2 = send(stage.at[h, qd, 0], ry.at[h, 1, 0], dev[3])
        s1[h] += [a2, b2]
    for h in range(2):
        u, dev = us[h]
        fill(h, mod4(u + 1), 0)
        fill(h, mod4(u - 1), 1)
        fill(h, u, 0)
        fill(h, u, 1)

    def add2(dst, a, b):
        @pl.loop(0, 4)
        def _(o):
            dst[o] = (a[o].astype(F32) + b[o].astype(F32)).astype(BF16)

    tile(0)
    tile(1)
    for h in range(2):
        u, dev = us[h]
        a1, b1, a2, b2 = s1[h]
        a1.wait_recv()
        add2(cb.at[h, 0], stage.at[h, mod4(u + 1), 0], rx.at[h, 0])
        a3 = send(cb.at[h, 0], ry.at[h, 0, 0], dev[1])
        b1.wait_recv()
        add2(cb.at[h, 1], stage.at[h, mod4(u - 1), 1], rx.at[h, 1])
        b3 = send(cb.at[h, 1], ry.at[h, 1, 1], dev[3])
        s1[h] += [a3, b3]
    tile(2)
    s2 = [None, None]
    for h in range(2):
        u, dev = us[h]
        w, wdev = ws[h]
        a1, b1, a2, b2, a3, b3 = s1[h]
        for ab, pair in ((0, (a3, b2)), (1, (a2, b3))):
            for c in pair:
                c.wait_recv()

            @pl.loop(0, 4)
            def _(o):
                r1[h, o, ab] = (
                    stage[h, u, ab, o].astype(F32) + ry[h, 0, ab, o].astype(F32) + ry[h, 1, ab, o].astype(F32)
                ).astype(BF16)
        s2[h] = [send(r1.at[h, mod4(w + d)], ry2.at[h, d], wdev[d]) for d in (1, 3, 2)]
    tile(3)
    for h in range(2):
        w, wdev = ws[h]
        for c in s2[h]:
            c.wait_recv()
        for ab in range(2):
            total = r1[h, w, ab].astype(F32)
            for d in (1, 2, 3):
                total = total + ry2[h, d, ab].astype(F32)
            gsum[pl.ds((h * 2 + ab) * BS, BS), :] = total * GRAD_SCALE

    g1 = [None, None]
    for h in range(2):
        u, dev = us[h]

        @pl.loop(0, 16)
        def _(j):
            rows = jnp.concatenate([gsum[pl.ds(quarter * 32 + h * 16 + j, 4, stride=BS), :] for quarter in range(4)], axis=0)
            g16[:, pl.ds(pl.multiple_of(h * 2048 + j * BS, BS), BS)] = rows
            agg[h, u, :, pl.ds(pl.multiple_of(j * BS, BS), BS)] = rows.astype(BF16)
        own = agg.at[h, u]
        g1[h] = [send(own, own, dev[d]) for d in (1, 3, 2)]

    def adam(g, m0, v0):
        m = BETA_ONE * m0 + (1.0 - BETA_ONE) * g
        v = BETA_TWO * v0 + (1.0 - BETA_TWO) * g * g
        return m, v

    for h in range(2):
        for c in m2[h]:
            c.wait_recv()
    d1 = [None, None]
    for h in range(2):
        u, dev = us[h]
        w, wdev = ws[h]

        @pl.loop(0, 16)
        def _(j):
            here = pl.ds(pl.multiple_of(h * 2048 + j * BS, BS), BS)
            parts = []
            for hm in range(2):
                got = sbm[hm, ws[hm][0], :, here].astype(F32)
                for d in (1, 2, 3):
                    got = got + rbm[hm, d, :, here].astype(F32)
                parts.append(got)
            m0 = jnp.concatenate([p[0:8] for p in parts], axis=0)
            v0 = jnp.concatenate([p[8:16] for p in parts], axis=0)
            m, v = adam(g16[:, here], m0, v0)
            new = cur[:, here] - LEARN_RATE * (m / CORRECT_ONE) / (jnp.sqrt(v / CORRECT_TWO) + EPSILON)
            gath[h, w, u, :, pl.ds(pl.multiple_of(j * BS, BS), BS)] = new.astype(BF16)
        own = gath.at[h, w, u]
        d1[h] = [send(own, own, dev[d]) for d in (1, 3, 2)]

    g2, d2 = [None, None], [None, None]
    for h in range(2):
        for c in g1[h]:
            c.wait_recv()

        @pl.loop(0, 4)
        def _(j):
            here = pl.ds(pl.multiple_of(j * 512, 512), 512)
            x = agg[h, :, :, here].reshape(64, 512)
            sbg[h, :, :, here] = jnp.dot(sel_g[h], x, preferred_element_type=F32).astype(BF16).reshape(4, 32, 512)
    for h in range(2):
        w, dev = ws[h]
        for c in d1[h]:
            c.wait_recv()
        lo, hi = gath.at[h, w, pl.ds(0, 2)], gath.at[h, w, pl.ds(2, 2)]
        d2[h] = [send(lo, lo, dev[1]), send(hi, hi, dev[3])]
    for h in range(2):
        w, dev = ws[h]
        g2[h] = [send(sbg.at[h, mod4(w + d)], rbg.at[h, d], dev[d]) for d in (1, 3, 2)]
        lo, hi = gath.at[h, w, pl.ds(0, 2)], gath.at[h, w, pl.ds(2, 2)]
        d2[h] += [send(hi, hi, dev[1]), send(lo, lo, dev[3])]
    tile(4)
    for h in range(2):
        w, dev = ws[h]
        d2[h][0].wait_recv()
        piece = gath.at[h, mod4(w - 1), pl.ds(0, 2)]
        f_up = send(piece, piece, dev[1])
        d2[h][1].wait_recv()
        piece = gath.at[h, mod4(w + 1), pl.ds(2, 2)]
        f_dn = send(piece, piece, dev[3])
        d2[h] += [f_up, f_dn]
    tile(5)
    for h in range(2):
        w, dev = ws[h]
        for c in g2[h]:
            c.wait_recv()

        @pl.loop(0, 16)
        def _(j):
            here = pl.ds(pl.multiple_of(j * BS, BS), BS)
            got = sbg[h, w, :, here].astype(F32)
            for d in (1, 2, 3):
                got = got + rbg[h, d, :, here].astype(F32)
            for quarter in range(4):
                lanes = pl.ds(pl.multiple_of(quarter * 4096 + h * 2048 + j * BS, BS), BS)
                m0, v0 = mbuf[:, lanes], vbuf[:, lanes]
                m, v = adam(got[quarter * 8:quarter * 8 + 8], m0, v0)
                mnew[:, lanes] = jnp.where(filled, m, m0)
                vnew[:, lanes] = jnp.where(filled, v, v0)
    out_m = local_copy(mnew, first_out, 6)
    out_v = local_copy(vnew, second_out, 7)
    tile(6)
    outs = []
    for h in range(2):
        for c in d2[h][2:]:
            c.wait_recv()

        @pl.loop(0, 4)
        def _(j):
            x = gath[h, :, :, :, pl.ds(pl.multiple_of(j * 512, 512), 512)].reshape(256, 512)
            y = jnp.dot(sel_d[h], x, preferred_element_type=F32).astype(BF16)
            for quarter in range(4):
                lanes = pl.ds(pl.multiple_of(quarter * 4096 + h * 2048 + j * 512, 512), 512)
                dnew[:, lanes] = y[quarter * 64:(quarter + 1) * 64]
        for quarter in range(4):
            lanes = pl.ds(quarter * 4096 + h * 2048, 2048)
            c = pltpu.make_async_copy(dnew.at[:, lanes], deltas_out.at[:, lanes], dsem.at[h * 4 + quarter])
            c.start()
            outs.append(c)
    for c in sent:
        c.wait_send()
    out_m.wait()
    out_v.wait()
    out_copy(TILES - 2, (TILES - 2) % 2).wait()
    out_copy(TILES - 1, (TILES - 1) % 2).wait()
    for c in outs:
        c.wait()


def local(hidden_act, cotangent, weight, deltas, block_ids, owners, first_moment, second_moment):
    any_spec = pl.BlockSpec(memory_space=pl.ANY)
    vm_spec = pl.BlockSpec(memory_space=pltpu.VMEM)
    V = pltpu.VMEM
    outs = pl.pallas_call(
        kernel,
        out_shape=(
            jax.ShapeDtypeStruct((TOK, FFL), BF16),
            jax.ShapeDtypeStruct((NBL, BS * BS), BF16),
            jax.ShapeDtypeStruct((CAP, BS * BS), F32),
            jax.ShapeDtypeStruct((CAP, BS * BS), F32),
        ),
        in_specs=[any_spec] * 4 + [vm_spec] * 2 + [any_spec] * 2,
        out_specs=(any_spec,) * 4,
        scratch_shapes=[
            V((TOK, D), BF16),
            V((TOK, FFL), BF16),
            V((FFL, TOK), BF16),
            V((RB * CB, BS, BS), BF16),
            V((2, TILE, D), BF16),
            V((NBL, BS * BS), BF16),
            V((NBL + 1, BS, BS), F32),
            V((2, 4, 2, 4, BS, BS), BF16),
            V((2, 2, 4, BS, BS), BF16),
            V((2, 2, 2, 4, BS, BS), BF16),
            V((2, 2, 4, BS, BS), BF16),
            V((2, 4, 2, BS, BS), BF16),
            V((2, 4, 2, BS, BS), BF16),
            V((4 * BS, BS), F32),
            V((2, 2, 4, 16, 4096), BF16),
            V((2, 4, 16, 4096), BF16),
            V((2, 4, 16, 4096), BF16),
            V((2, 4, 16, 2048), BF16),
            V((2, 4, 32, 2048), BF16),
            V((2, 4, 32, 2048), BF16),
            V((2, 4, 4, 16, 2048), BF16),
            V((16, 4096), F32),
            V((16, 4096), F32),
            V((CAP, BS * BS), F32),
            V((CAP, BS * BS), F32),
            V((CAP, BS * BS), F32),
            V((CAP, BS * BS), F32),
            V((NBL, BS * BS), BF16),
            V((2, TOK, TILE), BF16),
            V((8, 512), I32),
            pltpu.SMEM((8, 512), I32),
            V((2, 2, 64, 64), BF16),
            V((2, 128, 64), BF16),
            V((2, 256, 256), BF16),
            pltpu.SemaphoreType.DMA((8,)),
            pltpu.SemaphoreType.DMA((2,)),
            pltpu.SemaphoreType.DMA((2,)),
            pltpu.SemaphoreType.DMA((8,)),
            pltpu.SemaphoreType.DMA((N_REMOTE,)),
            pltpu.SemaphoreType.DMA((N_REMOTE,)),
        ],
        compiler_params=pltpu.CompilerParams(
            collective_id=0, has_side_effects=True, vmem_limit_bytes=60 * 1024 * 1024),
        cost_estimate=pl.CostEstimate(flops=15 * 10**9, bytes_accessed=25 * 10**6, transcendentals=0),
    )(
        cotangent, hidden_act, weight, deltas,
        block_ids.reshape(1, NBL), owners.reshape(1, NBL), first_moment[0], second_moment[0],
    )
    input_grad, new_deltas, new_first, new_second = outs
    return (input_grad, new_deltas, new_first[None], new_second[None])


def solution(mesh):
    in_specs = (
        P("dp", "mp"),
        P("dp", "mp"),
        P("mp", None),
        P("mp", None),
        P("mp"),
        P("mp", None),
        P("mp", "dp", None),
        P("mp", "dp", None),
    )
    out_specs = (P("dp", "mp"), P("mp", None), P("mp", "dp", None), P("mp", "dp", None))
    return jax.shard_map(local, mesh=mesh, in_specs=in_specs, out_specs=out_specs, check_vma=False)
```

time: 103 us -> 91.4 us (0.89)
  Pallas kernels: 93.2 us -> 84.7 us
  local copies, waits for them, and re-layouts: 9.45 us -> 5.96 us
    pallas_call x1, Pallas kernels: 93.2 us -> 84.7 us  [local(): pl.pallas_call(kernel, out_shape=(jax.ShapeDtypeStruct((TOK, FFL), BF16),...]
    unnamed x11 -> x10, local copies, waits for them, and re-layouts: 9.45 us -> 5.96 us
where the time goes in v2:
time: 91.4 us; the launch traced here: 91.3 us
  Pallas kernels  84.7 us (93%)
  local copies, waits for them, and re-layouts  5.96 us (7%)
    pallas_call x1, Pallas kernels, local(): pl.pallas_call(kernel, out_shape=(jax.ShapeDtypeStruct((TOK, FFL), BF16),...  84.7 us
    unnamed x10, local copies, waits for them, and re-layouts  5.96 us

profile of v2, /device:TPU:0, one launch (start us, length us, event | category | flops | bytes accessed | tf_op | source)
XLA Modules:
  0.0 91.3 jit_solution(2093809480623675341)
XLA Ops:
  0.6 84.7 %shard_map.111 = (bf16[512,1792]{1,0:T(8,128)(2,1)}, bf16[64,16384]{1,0:T(8,128)(2,1)}, f32[8,16384]{1,0:T(8,128)}, f32[8,16384]{1,0:T(8,128)}) custom-call(bf16[512,512]{1,0:T(8,128)(2,1)} %cot.1, bf16[512,1792]{1,0:T(8,128)(2,1)} %hid.1, bf16[1792,4096]{1,0:T(8,128)(2,1)} %weight.1, bf16[64,16384]{1,0:T(8,128)(2,1)} %deltas.1, s32[1,64]{1,0:T(1,128)} %bitcast.10, ...), custom_call_target="tpu_custom_call" | custom-call | flops 15000000512 | bytes 25000000 | tf_op jit(solution)/shard_map/pallas_call | solution.py:497
  85.3 0.0 copy-start
  85.3 3.0 %copy.16 = bf16[512,1792]{1,0:T(8,128)(2,1)} copy(bf16[512,1792]{1,0:T(8,128)(2,1)} %get-tuple-element.16) | data formatting | bytes 3670016
  88.3 0.0 copy-done
  88.3 0.0 copy-start.2
  88.3 0.0 copy-start.1
  88.3 1.3 %copy.17 = bf16[64,16384]{1,0:T(8,128)(2,1)} copy(bf16[64,16384]{1,0:T(8,128)(2,1)S(1)} %copy-done) | data formatting | bytes 4194304
  89.6 0.1 copy-done.2
  89.7 0.8 copy.18
  90.5 0.0 copy-done.1
  90.5 0.8 copy.19
Async XLA Ops:
  85.3 3.0 %copy-start = (bf16[64,16384]{1,0:T(8,128)(2,1)S(1)}, bf16[64,16384]{1,0:T(8,128)(2,1)}, u32[]{:S(2)}) copy-start(bf16[64,16384]{1,0:T(8,128)(2,1)} %get-tuple-element.17) | copy-start | bytes 6291460
  88.3 1.4 %copy-start.2 = (f32[8,16384]{1,0:T(8,128)S(1)}, f32[8,16384]{1,0:T(8,128)}, u32[]{:S(2)}) copy-start(f32[8,16384]{1,0:T(8,128)} %get-tuple-element.10) | copy-start | bytes 1572868
  88.3 2.2 %copy-start.1 = (f32[8,16384]{1,0:T(8,128)S(1)}, f32[8,16384]{1,0:T(8,128)}, u32[]{:S(2)}) copy-start(f32[8,16384]{1,0:T(8,128)} %get-tuple-element.11) | copy-start | bytes 1572868

commit v3 on v2

--- a/solution.py
+++ b/solution.py
@@ -29,7 +29,7 @@
 
 MESH = pl.DeviceIdType.MESH
 BF16, F32, I32 = jnp.bfloat16, jnp.float32, jnp.int32
-N_REMOTE = 80
+N_REMOTE = 96
 
 
 def mod4(v):
@@ -39,7 +39,7 @@
 def kernel(
     cot, hid, weight, deltas, ids_row, own_row, first, second,
     grad_out, deltas_out, first_out, second_out,
-    cbuf, hbuf, ht, dense, wbuf, drow, dblk, stage, rx, ry, cb, r1, ry2, gsum,
+    cbuf, hbuf, ht, dense, wbuf, drow, dwide, dblk, stage, rx, ry, cb, r1, ry2, gsum,
     agm, sbm, rbm, agg, sbg, rbg, gath, g16, cur, mbuf, vbuf, mnew, vnew, dnew, obuf, tab, stab,
     sel_m, sel_g, sel_d, lsem, wsem, osem, dsem, ssem, rsem,
 ):
@@ -166,21 +166,21 @@
         rows = pl.ds(pl.multiple_of(i * TILE, TILE), TILE)
         ht[rows, :] = hbuf[:, rows].T
 
-    def products(z, c, half, width):
+    def products(z, c, half):
         first_col = (z * 2 + c) * 4 + half * 2
-        where = col(z, c, half, width)
-
-        @pl.loop(0, TILES)
-        def _(i):
-            rows = pl.ds(pl.multiple_of(i * TILE, TILE), TILE)
-            g = jnp.dot(ht[rows, :], cbuf[:, where], preferred_element_type=F32).astype(BF16)
-            for r in range(2):
-                for k in range(width // BS):
-                    dense[(i * 2 + r) * CB + first_col + k] = g[r * BS:(r + 1) * BS, k * BS:(k + 1) * BS]
+        g = jnp.dot(ht[...], cbuf[:, col(z, c, half)], preferred_element_type=F32).astype(BF16)
+        for r in range(RB):
+            for k in range(2):
+                dense[r * CB + first_col + k] = g[r * BS:(r + 1) * BS, k * BS:(k + 1) * BS]
+
+    def both_products(z, c):
+        @pl.loop(0, 2)
+        def _(half):
+            products(z, c, half)
 
     mate_core = 1 - core
     zu, zd, zo = mod4(zz + 1), mod4(zz - 1), mod4(zz + 2)
-    products(zz, core, 0, 512)
+    both_products(zz, core)
     for h in range(2):
         u, dev = us[h]
         m1[h][0].wait_recv()
@@ -191,19 +191,19 @@
         f_dn = send(piece, piece, dev[3])
         m1[h] += [f_up, f_dn]
     to_mate.wait_recv()
-    products(zz, mate_core, 0, 512)
+    both_products(zz, mate_core)
     up_a.wait_recv()
     fw_a = share(col(zd, core, 0), z_up)
     m_da = share(col(zd, core, 0), mate)
     dn_b.wait_recv()
     fw_b = share(col(zu, core, 1), z_dn)
     m_ub = share(col(zu, core, 1), mate)
-    products(zd, core, 0, 256)
-    products(zu, core, 1, 256)
+    products(zd, core, 0)
+    products(zu, core, 1)
     m_da.wait_recv()
-    products(zd, mate_core, 0, 256)
+    products(zd, mate_core, 0)
     m_ub.wait_recv()
-    products(zu, mate_core, 1, 256)
+    products(zu, mate_core, 1)
 
     m2 = [None, None]
     for h in range(2):
@@ -225,12 +225,12 @@
     m_db = share(col(zd, core, 1), mate)
     dn_a.wait_recv()
     m_ua = share(col(zu, core, 0), mate)
-    products(zd, core, 1, 256)
-    products(zu, core, 0, 256)
+    products(zd, core, 1)
+    products(zu, core, 0)
     m_db.wait_recv()
-    products(zd, mate_core, 1, 256)
+    products(zd, mate_core, 1)
     m_ua.wait_recv()
-    products(zu, mate_core, 0, 256)
+    products(zu, mate_core, 0)
 
     cp_dr.wait()
     rc = lax.broadcasted_iota(I32, (16, NBL), 0)
@@ -247,22 +247,25 @@
             rows = rows + jnp.dot(pick, drow[:, there], preferred_element_type=F32)
         cur[:, here] = rows
 
-    by_row = dblk.reshape((NBL + 1) * BS, BS)
 
     @pl.loop(0, BS)
     def _(r):
-        by_row[pl.ds(r, NBL, stride=BS), :] = drow[:, pl.ds(pl.multiple_of(r * BS, BS), BS)].astype(F32)
-
-    dblk[NBL] = jnp.zeros((BS, BS), F32)
+        dwide[pl.ds(r, NBL, stride=BS), :] = drow[:, pl.ds(pl.multiple_of(r * BS, BS), BS)].astype(F32)
+
+    @pl.loop(0, NBL)
+    def _(k):
+        dblk[k] = dwide[pl.ds(pl.multiple_of(k * BS, BS), BS), :].astype(BF16)
+
+    dblk[NBL] = jnp.zeros((BS, BS), BF16)
 
     fw_a.wait_recv()
     m_oa = share(col(zo, core, 0), mate)
     fw_b.wait_recv()
     m_ob = share(col(zo, core, 1), mate)
-    products(zo, core, 0, 512)
+    both_products(zo, core)
     m_oa.wait_recv()
     m_ob.wait_recv()
-    products(zo, mate_core, 0, 512)
+    both_products(zo, mate_core)
     cp_tab.wait()
 
     def out_copy(n, slot):
@@ -280,91 +283,88 @@
             for r in range(2):
                 k = stab[0, (n * 2 + r) * CB + c]
                 cols = pl.ds(pl.multiple_of(c * BS, BS), BS)
-                add = dblk[k]
-                old = wbuf[slot, r * BS:(r + 1) * BS, cols]
-                wbuf[slot, r * BS:(r + 1) * BS, cols] = (old.astype(F32) + add).astype(BF16)
+                wbuf[slot, r * BS:(r + 1) * BS, cols] += dblk[k]
 
         if n >= 2:
             out_copy(n - 2, slot).wait()
 
-        @pl.loop(0, 2)
-        def _(m):
-            rows = pl.ds(pl.multiple_of(m * 256, 256), 256)
-            obuf[slot, rows, :] = lax.dot_general(
-                cbuf[rows, :], wbuf[slot], (((1,), (1,)), ((), ())), preferred_element_type=F32).astype(BF16)
+        obuf[slot] = lax.dot_general(
+            cbuf[...], wbuf[slot], (((1,), (1,)), ((), ())), preferred_element_type=F32).astype(BF16)
 
         out_copy(n, slot).start()
 
-    def fill(h, quarter, ab):
-        @pl.loop(0, 4)
-        def _(o):
+    def fill(h, quarter, chunk, ab):
+        for e in range(2):
+            o = mod4(ws[h][0] + 2 - 2 * chunk - e)
             dev = o * 4 + quarter if h else quarter * 4 + o
-            stage[h, quarter, ab, o] = dense[stab[1, dev * 4 + h * 2 + ab]]
-
-    s1 = [None, None]
-    for h in range(2):
-        u, dev = us[h]
-        opp = mod4(u + 2)
-        fill(h, opp, 0)
-        a1 = send(stage.at[h, opp, 0], rx.at[h, 0], dev[1])
-        fill(h, opp, 1)
-        b1 = send(stage.at[h, opp, 1], rx.at[h, 1], dev[3])
-        s1[h] = [a1, b1]
-    for h in range(2):
-        u, dev = us[h]
-        qu, qd = mod4(u + 1), mod4(u - 1)
-        fill(h, qu, 1)
-        a2 = send(stage.at[h, qu, 1], ry.at[h, 0, 1], dev[1])
-        fill(h, qd, 0)
-        b2 = send(stage.at[h, qd, 0], ry.at[h, 1, 0], dev[3])
-        s1[h] += [a2, b2]
-    for h in range(2):
-        u, dev = us[h]
-        fill(h, mod4(u + 1), 0)
-        fill(h, mod4(u - 1), 1)
-        fill(h, u, 0)
-        fill(h, u, 1)
-
-    def add2(dst, a, b):
-        @pl.loop(0, 4)
-        def _(o):
-            dst[o] = (a[o].astype(F32) + b[o].astype(F32)).astype(BF16)
+            stage[h, quarter, chunk, ab, e] = dense[stab[1, dev * 4 + h * 2 + ab]]
+
+    s1 = {}
+    for ch in range(2):
+        for h in range(2):
+            u, dev = us[h]
+            opp = mod4(u + 2)
+            fill(h, opp, ch, 0)
+            s1[h, ch, 0] = send(stage.at[h, opp, ch, 0], rx.at[h, ch, 0], dev[1])
+            fill(h, opp, ch, 1)
+            s1[h, ch, 1] = send(stage.at[h, opp, ch, 1], rx.at[h, ch, 1], dev[3])
+        for h in range(2):
+            u, dev = us[h]
+            qu, qd = mod4(u + 1), mod4(u - 1)
+            fill(h, qu, ch, 1)
+            s1[h, ch, 2] = send(stage.at[h, qu, ch, 1], ry.at[h, ch, 0, 1], dev[1])
+            fill(h, qd, ch, 0)
+            s1[h, ch, 3] = send(stage.at[h, qd, ch, 0], ry.at[h, ch, 1, 0], dev[3])
+    for ch in range(2):
+        for h in range(2):
+            u, dev = us[h]
+            fill(h, mod4(u + 1), ch, 0)
+            fill(h, mod4(u - 1), ch, 1)
+            fill(h, u, ch, 0)
+            fill(h, u, ch, 1)
+
+    def combine(ch):
+        for h in range(2):
+            u, dev = us[h]
+            for ab, q, d in ((0, mod4(u + 1), 1), (1, mod4(u - 1), 3)):
+                s1[h, ch, ab].wait_recv()
+                for e in range(2):
+                    cb[h, ch, ab, e] = (
+                        stage[h, q, ch, ab, e].astype(F32) + rx[h, ch, ab, e].astype(F32)).astype(BF16)
+                s1[h, ch, 4 + ab] = send(cb.at[h, ch, ab], ry.at[h, ch, ab, ab], dev[d])
+
+    s2 = [[], []]
+
+    def second(ch):
+        for h in range(2):
+            u, dev = us[h]
+            w, wdev = ws[h]
+            for ab, pair in ((0, (4, 3)), (1, (2, 5))):
+                for c in pair:
+                    s1[h, ch, c].wait_recv()
+                for e in range(2):
+                    r1[h, ch, e, ab] = (
+                        stage[h, u, ch, ab, e].astype(F32) + ry[h, ch, 0, ab, e].astype(F32)
+                        + ry[h, ch, 1, ab, e].astype(F32)).astype(BF16)
+            for e in range(2):
+                d = (2 - 2 * ch - e) % 4
+                if d:
+                    s2[h].append(send(r1.at[h, ch, e], ry2.at[h, d], wdev[d]))
 
     tile(0)
+    combine(0)
     tile(1)
-    for h in range(2):
-        u, dev = us[h]
-        a1, b1, a2, b2 = s1[h]
-        a1.wait_recv()
-        add2(cb.at[h, 0], stage.at[h, mod4(u + 1), 0], rx.at[h, 0])
-        a3 = send(cb.at[h, 0], ry.at[h, 0, 0], dev[1])
-        b1.wait_recv()
-        add2(cb.at[h, 1], stage.at[h, mod4(u - 1), 1], rx.at[h, 1])
-        b3 = send(cb.at[h, 1], ry.at[h, 1, 1], dev[3])
-        s1[h] += [a3, b3]
+    combine(1)
+    second(0)
     tile(2)
-    s2 = [None, None]
-    for h in range(2):
-        u, dev = us[h]
-        w, wdev = ws[h]
-        a1, b1, a2, b2, a3, b3 = s1[h]
-        for ab, pair in ((0, (a3, b2)), (1, (a2, b3))):
-            for c in pair:
-                c.wait_recv()
-
-            @pl.loop(0, 4)
-            def _(o):
-                r1[h, o, ab] = (
-                    stage[h, u, ab, o].astype(F32) + ry[h, 0, ab, o].astype(F32) + ry[h, 1, ab, o].astype(F32)
-                ).astype(BF16)
-        s2[h] = [send(r1.at[h, mod4(w + d)], ry2.at[h, d], wdev[d]) for d in (1, 3, 2)]
+    second(1)
     tile(3)
     for h in range(2):
         w, wdev = ws[h]
         for c in s2[h]:
             c.wait_recv()
         for ab in range(2):
-            total = r1[h, w, ab].astype(F32)
+            total = r1[h, 1, 0, ab].astype(F32)
             for d in (1, 2, 3):
                 total = total + ry2[h, d, ab].astype(F32)
             gsum[pl.ds((h * 2 + ab) * BS, BS), :] = total * GRAD_SCALE
@@ -511,12 +511,13 @@
             V((RB * CB, BS, BS), BF16),
             V((2, TILE, D), BF16),
             V((NBL, BS * BS), BF16),
-            V((NBL + 1, BS, BS), F32),
-            V((2, 4, 2, 4, BS, BS), BF16),
-            V((2, 2, 4, BS, BS), BF16),
-            V((2, 2, 2, 4, BS, BS), BF16),
-            V((2, 2, 4, BS, BS), BF16),
-            V((2, 4, 2, BS, BS), BF16),
+            V((NBL * BS, BS), F32),
+            V((NBL + 1, BS, BS), BF16),
+            V((2, 4, 2, 2, 2, BS, BS), BF16),
+            V((2, 2, 2, 2, BS, BS), BF16),
+            V((2, 2, 2, 2, 2, BS, BS), BF16),
+            V((2, 2, 2, 2, BS, BS), BF16),
+            V((2, 2, 2, 2, BS, BS), BF16),
             V((2, 4, 2, BS, BS), BF16),
             V((4 * BS, BS), F32),
             V((2, 2, 4, 16, 4096), BF16),

time: 91.4 us -> 87.6 us (0.958)
  Pallas kernels: 84.7 us -> 80.8 us
    pallas_call x1, Pallas kernels: 84.7 us -> 80.8 us  [local(): pl.pallas_call(kernel, out_shape=(jax.ShapeDtypeStruct((TOK, FFL), BF16),...]
where the time goes in v3:
time: 87.6 us; the launch traced here: 87.4 us
  Pallas kernels  80.8 us (92%)
  local copies, waits for them, and re-layouts  5.96 us (7%)
    pallas_call x1, Pallas kernels, local(): pl.pallas_call(kernel, out_shape=(jax.ShapeDtypeStruct((TOK, FFL), BF16),...  80.8 us
    unnamed x10, local copies, waits for them, and re-layouts  5.96 us

profile of v3, /device:TPU:0, one launch (start us, length us, event | category | flops | bytes accessed | tf_op | source)
XLA Modules:
  0.0 87.4 jit_solution(6472321370381050021)
XLA Ops:
  0.6 80.8 %shard_map.111 = (bf16[512,1792]{1,0:T(8,128)(2,1)}, bf16[64,16384]{1,0:T(8,128)(2,1)}, f32[8,16384]{1,0:T(8,128)}, f32[8,16384]{1,0:T(8,128)}) custom-call(bf16[512,512]{1,0:T(8,128)(2,1)} %cot.1, bf16[512,1792]{1,0:T(8,128)(2,1)} %hid.1, bf16[1792,4096]{1,0:T(8,128)(2,1)} %weight.1, bf16[64,16384]{1,0:T(8,128)(2,1)} %deltas.1, s32[1,64]{1,0:T(1,128)} %bitcast.10, ...), custom_call_target="tpu_custom_call" | custom-call | flops 15000000512 | bytes 25000000 | tf_op jit(solution)/shard_map/pallas_call | solution.py:497
  81.5 0.0 copy-start
  81.5 3.0 %copy.16 = bf16[512,1792]{1,0:T(8,128)(2,1)} copy(bf16[512,1792]{1,0:T(8,128)(2,1)} %get-tuple-element.16) | data formatting | bytes 3670016
  84.5 0.0 copy-done
  84.5 0.0 copy-start.2
  84.5 0.0 copy-start.1
  84.5 1.3 %copy.17 = bf16[64,16384]{1,0:T(8,128)(2,1)} copy(bf16[64,16384]{1,0:T(8,128)(2,1)S(1)} %copy-done) | data formatting | bytes 4194304
  85.8 0.1 copy-done.2
  85.8 0.8 copy.18
  86.6 0.0 copy-done.1
  86.6 0.8 copy.19
Async XLA Ops:
  81.5 3.0 %copy-start = (bf16[64,16384]{1,0:T(8,128)(2,1)S(1)}, bf16[64,16384]{1,0:T(8,128)(2,1)}, u32[]{:S(2)}) copy-start(bf16[64,16384]{1,0:T(8,128)(2,1)} %get-tuple-element.17) | copy-start | bytes 6291460
  84.5 1.4 %copy-start.2 = (f32[8,16384]{1,0:T(8,128)S(1)}, f32[8,16384]{1,0:T(8,128)}, u32[]{:S(2)}) copy-start(f32[8,16384]{1,0:T(8,128)} %get-tuple-element.10) | copy-start | bytes 1572868
  84.5 2.2 %copy-start.1 = (f32[8,16384]{1,0:T(8,128)S(1)}, f32[8,16384]{1,0:T(8,128)}, u32[]{:S(2)}) copy-start(f32[8,16384]{1,0:T(8,128)} %get-tuple-element.11) | copy-start | bytes 1572868

commit v4 on v3

--- a/solution.py
+++ b/solution.py
@@ -30,6 +30,8 @@
 MESH = pl.DeviceIdType.MESH
 BF16, F32, I32 = jnp.bfloat16, jnp.float32, jnp.int32
 N_REMOTE = 96
+VMEM_MAIN = 56 * 1024 * 1024
+OUT = pltpu.VMEM
 
 
 def mod4(v):
@@ -38,10 +40,10 @@
 
 def kernel(
     cot, hid, weight, deltas, ids_row, own_row, first, second,
-    grad_out, deltas_out, first_out, second_out,
+    grad_out, gath, mnew, vnew,
     cbuf, hbuf, ht, dense, wbuf, drow, dwide, dblk, stage, rx, ry, cb, r1, ry2, gsum,
-    agm, sbm, rbm, agg, sbg, rbg, gath, g16, cur, mbuf, vbuf, mnew, vnew, dnew, obuf, tab, stab,
-    sel_m, sel_g, sel_d, lsem, wsem, osem, dsem, ssem, rsem,
+    agm, sbm, rbm, agg, sbg, rbg, g16, cur, mbuf, vbuf, tab, stab,
+    sel_m, sel_g, lsem, wsem, ssem, rsem,
 ):
     dp, mp = lax.axis_index("dp"), lax.axis_index("mp")
     xx, yy = dp // 4, lax.rem(dp, 4)
@@ -153,11 +155,6 @@
         rg = lax.broadcasted_iota(I32, (128, NBL), 0)
         cg = lax.broadcasted_iota(I32, (128, NBL), 1)
         sel_g[h] = one_hot((goes == dev_dest(rg >> 5) * CAP + (rg & 7)) & (((rg >> 3) & 3) == ((cg >> 2) & 3)))
-        rd = lax.broadcasted_iota(I32, (256, 256), 0)
-        cd = lax.broadcasted_iota(I32, (256, 256), 1)
-        group, mem = cd >> 6, (cd >> 4) & 3
-        dev = group * 4 + mem if h else mem * 4 + group
-        sel_d[h] = one_hot(((rd & 63) == dev * 4 + (cd & 3)) & ((rd >> 6) == ((cd >> 2) & 3)))
 
     cp_hid.wait()
 
@@ -232,32 +229,6 @@
     m_ua.wait_recv()
     products(zu, mate_core, 0)
 
-    cp_dr.wait()
-    rc = lax.broadcasted_iota(I32, (16, NBL), 0)
-    cc = lax.broadcasted_iota(I32, (16, NBL), 1)
-    my_row = cc == dp * 4 + (rc & 3)
-
-    @pl.loop(0, 8)
-    def _(j):
-        here = pl.ds(pl.multiple_of(j * 512, 512), 512)
-        rows = 0.0
-        for quarter in range(4):
-            there = pl.ds(pl.multiple_of(quarter * 4096 + j * 512, 512), 512)
-            pick = one_hot(my_row & ((rc >> 2) == quarter))
-            rows = rows + jnp.dot(pick, drow[:, there], preferred_element_type=F32)
-        cur[:, here] = rows
-
-
-    @pl.loop(0, BS)
-    def _(r):
-        dwide[pl.ds(r, NBL, stride=BS), :] = drow[:, pl.ds(pl.multiple_of(r * BS, BS), BS)].astype(F32)
-
-    @pl.loop(0, NBL)
-    def _(k):
-        dblk[k] = dwide[pl.ds(pl.multiple_of(k * BS, BS), BS), :].astype(BF16)
-
-    dblk[NBL] = jnp.zeros((BS, BS), BF16)
-
     fw_a.wait_recv()
     m_oa = share(col(zo, core, 0), mate)
     fw_b.wait_recv()
@@ -268,10 +239,6 @@
     both_products(zo, mate_core)
     cp_tab.wait()
 
-    def out_copy(n, slot):
-        return pltpu.make_async_copy(
-            obuf.at[slot], grad_out.at[:, pl.ds(pl.multiple_of(n * TILE, TILE), TILE)], osem.at[slot])
-
     def tile(n):
         slot = n % 2
         if n + 1 < TILES:
@@ -285,13 +252,8 @@
                 cols = pl.ds(pl.multiple_of(c * BS, BS), BS)
                 wbuf[slot, r * BS:(r + 1) * BS, cols] += dblk[k]
 
-        if n >= 2:
-            out_copy(n - 2, slot).wait()
-
-        obuf[slot] = lax.dot_general(
+        grad_out[:, pl.ds(n * TILE, TILE)] = lax.dot_general(
             cbuf[...], wbuf[slot], (((1,), (1,)), ((), ())), preferred_element_type=F32).astype(BF16)
-
-        out_copy(n, slot).start()
 
     def fill(h, quarter, chunk, ab):
         for e in range(2):
@@ -351,13 +313,39 @@
                 if d:
                     s2[h].append(send(r1.at[h, ch, e], ry2.at[h, d], wdev[d]))
 
+    cp_dr.wait()
+    rc = lax.broadcasted_iota(I32, (16, NBL), 0)
+    cc = lax.broadcasted_iota(I32, (16, NBL), 1)
+    my_row = cc == dp * 4 + (rc & 3)
+
+    @pl.loop(0, 8)
+    def _(j):
+        here = pl.ds(pl.multiple_of(j * 512, 512), 512)
+        rows = 0.0
+        for quarter in range(4):
+            there = pl.ds(pl.multiple_of(quarter * 4096 + j * 512, 512), 512)
+            pick = one_hot(my_row & ((rc >> 2) == quarter))
+            rows = rows + jnp.dot(pick, drow[:, there], preferred_element_type=F32)
+        cur[:, here] = rows
+
+
+    @pl.loop(0, BS)
+    def _(r):
+        dwide[pl.ds(r, NBL, stride=BS), :] = drow[:, pl.ds(pl.multiple_of(r * BS, BS), BS)].astype(F32)
+
+    @pl.loop(0, NBL)
+    def _(k):
+        dblk[k] = dwide[pl.ds(pl.multiple_of(k * BS, BS), BS), :].astype(BF16)
+
+    dblk[NBL] = jnp.zeros((BS, BS), BF16)
+
+    combine(0)
     tile(0)
-    combine(0)
+    combine(1)
     tile(1)
-    combine(1)
     second(0)
+    second(1)
     tile(2)
-    second(1)
     tile(3)
     for h in range(2):
         w, wdev = ws[h]
@@ -373,11 +361,14 @@
     for h in range(2):
         u, dev = us[h]
 
-        @pl.loop(0, 16)
-        def _(j):
-            rows = jnp.concatenate([gsum[pl.ds(quarter * 32 + h * 16 + j, 4, stride=BS), :] for quarter in range(4)], axis=0)
-            g16[:, pl.ds(pl.multiple_of(h * 2048 + j * BS, BS), BS)] = rows
-            agg[h, u, :, pl.ds(pl.multiple_of(j * BS, BS), BS)] = rows.astype(BF16)
+        @pl.loop(0, 4)
+        def _(jj):
+            for k in range(4):
+                j = jj * 4 + k
+                rows = jnp.concatenate(
+                    [gsum[pl.ds(quarter * 32 + h * 16 + j, 4, stride=BS), :] for quarter in range(4)], axis=0)
+                g16[:, pl.ds(pl.multiple_of(h * 2048 + j * BS, BS), BS)] = rows
+                agg[h, u, :, pl.ds(pl.multiple_of(j * BS, BS), BS)] = rows.astype(BF16)
         own = agg.at[h, u]
         g1[h] = [send(own, own, dev[d]) for d in (1, 3, 2)]
 
@@ -394,9 +385,9 @@
         u, dev = us[h]
         w, wdev = ws[h]
 
-        @pl.loop(0, 16)
+        @pl.loop(0, 4)
         def _(j):
-            here = pl.ds(pl.multiple_of(h * 2048 + j * BS, BS), BS)
+            here = pl.ds(pl.multiple_of(h * 2048 + j * 512, 512), 512)
             parts = []
             for hm in range(2):
                 got = sbm[hm, ws[hm][0], :, here].astype(F32)
@@ -407,7 +398,7 @@
             v0 = jnp.concatenate([p[8:16] for p in parts], axis=0)
             m, v = adam(g16[:, here], m0, v0)
             new = cur[:, here] - LEARN_RATE * (m / CORRECT_ONE) / (jnp.sqrt(v / CORRECT_TWO) + EPSILON)
-            gath[h, w, u, :, pl.ds(pl.multiple_of(j * BS, BS), BS)] = new.astype(BF16)
+            gath[h, w, u, :, pl.ds(pl.multiple_of(j * 512, 512), 512)] = new.astype(BF16)
         own = gath.at[h, w, u]
         d1[h] = [send(own, own, dev[d]) for d in (1, 3, 2)]
 
@@ -421,6 +412,8 @@
             here = pl.ds(pl.multiple_of(j * 512, 512), 512)
             x = agg[h, :, :, here].reshape(64, 512)
             sbg[h, :, :, here] = jnp.dot(sel_g[h], x, preferred_element_type=F32).astype(BF16).reshape(4, 32, 512)
+        w, dev = ws[h]
+        g2[h] = [send(sbg.at[h, mod4(w + d)], rbg.at[h, d], dev[d]) for d in (2, 1, 3)]
     for h in range(2):
         w, dev = ws[h]
         for c in d1[h]:
@@ -429,7 +422,6 @@
         d2[h] = [send(lo, lo, dev[1]), send(hi, hi, dev[3])]
     for h in range(2):
         w, dev = ws[h]
-        g2[h] = [send(sbg.at[h, mod4(w + d)], rbg.at[h, d], dev[d]) for d in (1, 3, 2)]
         lo, hi = gath.at[h, w, pl.ds(0, 2)], gath.at[h, w, pl.ds(2, 2)]
         d2[h] += [send(hi, hi, dev[1]), send(lo, lo, dev[3])]
     tile(4)
@@ -448,45 +440,54 @@
         for c in g2[h]:
             c.wait_recv()
 
-        @pl.loop(0, 16)
+        @pl.loop(0, 4)
         def _(j):
-            here = pl.ds(pl.multiple_of(j * BS, BS), BS)
+            here = pl.ds(pl.multiple_of(j * 512, 512), 512)
             got = sbg[h, w, :, here].astype(F32)
             for d in (1, 2, 3):
                 got = got + rbg[h, d, :, here].astype(F32)
             for quarter in range(4):
-                lanes = pl.ds(pl.multiple_of(quarter * 4096 + h * 2048 + j * BS, BS), BS)
+                lanes = pl.ds(pl.multiple_of(quarter * 4096 + h * 2048 + j * 512, 512), 512)
                 m0, v0 = mbuf[:, lanes], vbuf[:, lanes]
                 m, v = adam(got[quarter * 8:quarter * 8 + 8], m0, v0)
                 mnew[:, lanes] = jnp.where(filled, m, m0)
                 vnew[:, lanes] = jnp.where(filled, v, v0)
-    out_m = local_copy(mnew, first_out, 6)
-    out_v = local_copy(vnew, second_out, 7)
     tile(6)
-    outs = []
     for h in range(2):
         for c in d2[h][2:]:
             c.wait_recv()
+    for c in sent:
+        c.wait_send()
+
+
+def finish(grad, gath, mnew, vnew, grad_out, deltas_out, first_out, second_out, dnew, sel, sem):
+    copies = [pltpu.make_async_copy(mnew, first_out, sem.at[0]), pltpu.make_async_copy(vnew, second_out, sem.at[1])]
+    for k in range(4):
+        rows = pl.ds(k * 128, 128)
+        copies.append(pltpu.make_async_copy(grad.at[rows], grad_out.at[rows], sem.at[2 + k]))
+    for c in copies:
+        c.start()
+    rd = lax.broadcasted_iota(I32, (256, 256), 0)
+    cd = lax.broadcasted_iota(I32, (256, 256), 1)
+    group, mem = cd >> 6, (cd >> 4) & 3
+    for h in range(2):
+        dev = group * 4 + mem if h else mem * 4 + group
+        hit = ((rd & 63) == dev * 4 + (cd & 3)) & ((rd >> 6) == ((cd >> 2) & 3))
+        sel[...] = jnp.where(hit, 1.0, 0.0).astype(BF16)
 
         @pl.loop(0, 4)
         def _(j):
             x = gath[h, :, :, :, pl.ds(pl.multiple_of(j * 512, 512), 512)].reshape(256, 512)
-            y = jnp.dot(sel_d[h], x, preferred_element_type=F32).astype(BF16)
+            y = jnp.dot(sel[...], x, preferred_element_type=F32).astype(BF16)
             for quarter in range(4):
                 lanes = pl.ds(pl.multiple_of(quarter * 4096 + h * 2048 + j * 512, 512), 512)
                 dnew[:, lanes] = y[quarter * 64:(quarter + 1) * 64]
         for quarter in range(4):
             lanes = pl.ds(quarter * 4096 + h * 2048, 2048)
-            c = pltpu.make_async_copy(dnew.at[:, lanes], deltas_out.at[:, lanes], dsem.at[h * 4 + quarter])
+            c = pltpu.make_async_copy(dnew.at[:, lanes], deltas_out.at[:, lanes], sem.at[6 + h * 4 + quarter])
             c.start()
-            outs.append(c)
-    for c in sent:
-        c.wait_send()
-    out_m.wait()
-    out_v.wait()
-    out_copy(TILES - 2, (TILES - 2) % 2).wait()
-    out_copy(TILES - 1, (TILES - 1) % 2).wait()
-    for c in outs:
+            copies.append(c)
+    for c in copies:
         c.wait()
 
 
@@ -497,13 +498,13 @@
     outs = pl.pallas_call(
         kernel,
         out_shape=(
-            jax.ShapeDtypeStruct((TOK, FFL), BF16),
-            jax.ShapeDtypeStruct((NBL, BS * BS), BF16),
-            jax.ShapeDtypeStruct((CAP, BS * BS), F32),
-            jax.ShapeDtypeStruct((CAP, BS * BS), F32),
+            OUT((TOK, FFL), BF16),
+            OUT((2, 4, 4, 16, 2048), BF16),
+            OUT((CAP, BS * BS), F32),
+            OUT((CAP, BS * BS), F32),
         ),
         in_specs=[any_spec] * 4 + [vm_spec] * 2 + [any_spec] * 2,
-        out_specs=(any_spec,) * 4,
+        out_specs=(vm_spec,) * 4,
         scratch_shapes=[
             V((TOK, D), BF16),
             V((TOK, FFL), BF16),
@@ -526,35 +527,44 @@
             V((2, 4, 16, 2048), BF16),
             V((2, 4, 32, 2048), BF16),
             V((2, 4, 32, 2048), BF16),
-            V((2, 4, 4, 16, 2048), BF16),
             V((16, 4096), F32),
             V((16, 4096), F32),
             V((CAP, BS * BS), F32),
             V((CAP, BS * BS), F32),
-            V((CAP, BS * BS), F32),
-            V((CAP, BS * BS), F32),
-            V((NBL, BS * BS), BF16),
-            V((2, TOK, TILE), BF16),
             V((8, 512), I32),
             pltpu.SMEM((8, 512), I32),
             V((2, 2, 64, 64), BF16),
             V((2, 128, 64), BF16),
-            V((2, 256, 256), BF16),
             pltpu.SemaphoreType.DMA((8,)),
             pltpu.SemaphoreType.DMA((2,)),
-            pltpu.SemaphoreType.DMA((2,)),
-            pltpu.SemaphoreType.DMA((8,)),
             pltpu.SemaphoreType.DMA((N_REMOTE,)),
             pltpu.SemaphoreType.DMA((N_REMOTE,)),
         ],
         compiler_params=pltpu.CompilerParams(
-            collective_id=0, has_side_effects=True, vmem_limit_bytes=60 * 1024 * 1024),
+            collective_id=0, has_side_effects=True, vmem_limit_bytes=VMEM_MAIN),
         cost_estimate=pl.CostEstimate(flops=15 * 10**9, bytes_accessed=25 * 10**6, transcendentals=0),
     )(
         cotangent, hidden_act, weight, deltas,
         block_ids.reshape(1, NBL), owners.reshape(1, NBL), first_moment[0], second_moment[0],
     )
-    input_grad, new_deltas, new_first, new_second = outs
+    input_grad, new_deltas, new_first, new_second = pl.pallas_call(
+        finish,
+        out_shape=(
+            jax.ShapeDtypeStruct((TOK, FFL), BF16),
+            jax.ShapeDtypeStruct((NBL, BS * BS), BF16),
+            jax.ShapeDtypeStruct((CAP, BS * BS), F32),
+            jax.ShapeDtypeStruct((CAP, BS * BS), F32),
+        ),
+        in_specs=[any_spec, vm_spec, any_spec, any_spec],
+        out_specs=(any_spec,) * 4,
+        scratch_shapes=[
+            V((NBL, BS * BS), BF16),
+            V((256, 256), BF16),
+            pltpu.SemaphoreType.DMA((14,)),
+        ],
+        compiler_params=pltpu.CompilerParams(vmem_limit_bytes=16 * 1024 * 1024),
+        cost_estimate=pl.CostEstimate(flops=5 * 10**8, bytes_accessed=10**7, transcendentals=0),
+    )(*outs)
     return (input_grad, new_deltas, new_first[None], new_second[None])
 
 

time: 87.6 us -> 81.4 us (0.929)
  local copies, waits for them, and re-layouts: 5.96 us -> 0 us
    unnamed x10 -> x0, local copies, waits for them, and re-layouts: 5.96 us -> none
    pallas_call x1 -> x2, Pallas kernels: 80.8 us -> 80.3 us  [the longest x1 77.3 us: local(): pl.pallas_call(kernel, out_shape=(OUT((TOK, FFL), BF16), OUT((2, 4, 4, 16...]
where the time goes in v4:
time: 81.4 us; the launch traced here: 81.1 us
  Pallas kernels  80.3 us (99%)
    pallas_call x1, Pallas kernels, local(): pl.pallas_call(kernel, out_shape=(OUT((TOK, FFL), BF16), OUT((2, 4, 4, 16...  77.3 us
    pallas_call x1, Pallas kernels, local(): pl.pallas_call(finish, out_shape=(jax.ShapeDtypeStruct((TOK, FFL), BF16),...  3.01 us

profile of v4, /device:TPU:0, one launch (start us, length us, event | category | flops | bytes accessed | tf_op | source)
XLA Modules:
  0.0 81.1 jit_solution(14154682708911761345)
XLA Ops:
  0.6 77.3 %shard_map.111 = (bf16[512,1792]{1,0:T(8,128)(2,1)S(1)}, bf16[2,4,4,16,2048]{4,3,2,1,0:T(8,128)(2,1)S(1)}, f32[8,16384]{1,0:T(8,128)S(1)}, f32[8,16384]{1,0:T(8,128)S(1)}) custom-call(bf16[512,512]{1,0:T(8,128)(2,1)} %cot.1, bf16[512,1792]{1,0:T(8,128)(2,1)} %hid.1, bf16[1792,4096]{1,0:T(8,128)(2,1)} %weight.1, bf16[64,16384]{1,0:T(8,128)(2,1)} %deltas.1, ...), custom_call_target="tpu_custom_call" | custom-call | flops 15000000512 | bytes 25000000 | tf_op jit(solution)/shard_map/pallas_call | solution.py:498
  78.0 3.0 %shard_map.112 = (bf16[512,1792]{1,0:T(8,128)(2,1)}, bf16[64,16384]{1,0:T(8,128)(2,1)}, f32[8,16384]{1,0:T(8,128)}, f32[8,16384]{1,0:T(8,128)}) custom-call(bf16[512,1792]{1,0:T(8,128)(2,1)S(1)} %get-tuple-element.12.grad, bf16[2,4,4,16,2048]{4,3,2,1,0:T(8,128)(2,1)S(1)} %get-tuple-element.13.gath, f32[8,16384]{1,0:T(8,128)S(1)} %get-tuple-element.14.mnew, ...), custom_call_target="tpu_custom_call" | custom-call | flops 500000000 | bytes 10000000 | tf_op jit(solution)/shard_map/pallas_call | solution.py:550

commit v5 on v4

--- a/solution.py
+++ b/solution.py
@@ -73,8 +73,6 @@
         return pltpu.make_async_copy(
             weight.at[pl.ds(pl.multiple_of(n * TILE, TILE), TILE)], wbuf.at[slot], wsem.at[slot])
 
-    w_copy(0, 0).start()
-
     barrier = pltpu.get_barrier_semaphore()
     for dev in (*x_dev[1:], *y_dev[1:], z_up, z_dn, mate):
         pl.semaphore_signal(barrier, inc=1, device_id=dev, device_id_type=MESH)
@@ -157,6 +155,8 @@
         sel_g[h] = one_hot((goes == dev_dest(rg >> 5) * CAP + (rg & 7)) & (((rg >> 3) & 3) == ((cg >> 2) & 3)))
 
     cp_hid.wait()
+    for n in range(4):
+        w_copy(n, n).start()
 
     @pl.loop(0, TILES)
     def _(i):
@@ -189,6 +189,54 @@
         m1[h] += [f_up, f_dn]
     to_mate.wait_recv()
     both_products(zz, mate_core)
+    cp_dr.wait()
+    rc = lax.broadcasted_iota(I32, (16, NBL), 0)
+    cc = lax.broadcasted_iota(I32, (16, NBL), 1)
+    my_row = cc == dp * 4 + (rc & 3)
+
+    @pl.loop(0, 2)
+    def _(j):
+        here = pl.ds(pl.multiple_of(j * 2048, 2048), 2048)
+        rows = 0.0
+        for quarter in range(4):
+            there = pl.ds(pl.multiple_of(quarter * 4096 + j * 2048, 2048), 2048)
+            pick = one_hot(my_row & ((rc >> 2) == quarter))
+            rows = rows + jnp.dot(pick, drow[:, there], preferred_element_type=F32)
+        cur[:, here] = rows
+
+
+    @pl.loop(0, BS // 8)
+    def _(rr):
+        for k in range(8):
+            r = rr * 8 + k
+            dwide[pl.ds(r, NBL, stride=BS), :] = drow[:, pl.ds(pl.multiple_of(r * BS, BS), BS)].astype(F32)
+
+    @pl.loop(0, NBL // 8)
+    def _(k):
+        at = pl.multiple_of(k * 8, 8)
+        dblk[pl.ds(at, 8)] = dwide[pl.ds(at * BS, 8 * BS), :].astype(BF16).reshape(8, BS, BS)
+
+    dblk[NBL] = jnp.zeros((BS, BS), BF16)
+
+    def merge(n):
+        slot = n % 4
+        w_copy(n, slot).wait()
+
+        @pl.loop(0, CB // 8)
+        def _(c):
+            cols = pl.ds(pl.multiple_of(c * 8 * BS, 8 * BS), 8 * BS)
+            for r in range(2):
+                row = [dblk[stab[0, (n * 2 + r) * CB + c * 8 + j]] for j in range(8)]
+                wbuf[slot, r * BS:(r + 1) * BS, cols] += jnp.concatenate(row, axis=1)
+
+    def multiply(n):
+        grad_out[:, pl.ds(n * TILE, TILE)] = lax.dot_general(
+            cbuf[...], wbuf[n % 4], (((1,), (1,)), ((), ())), preferred_element_type=F32).astype(BF16)
+        if n + 4 < TILES:
+            w_copy(n + 4, n % 4).start()
+
+    cp_tab.wait()
+    merge(0)
     up_a.wait_recv()
     fw_a = share(col(zd, core, 0), z_up)
     m_da = share(col(zd, core, 0), mate)
@@ -207,14 +255,14 @@
         for c in m1[h][2:]:
             c.wait_recv()
 
-        @pl.loop(0, 8)
+        @pl.loop(0, 2)
         def _(j):
-            here = pl.ds(pl.multiple_of(j * 512, 512), 512)
+            here = pl.ds(pl.multiple_of(j * 2048, 2048), 2048)
             both = 0.0
             for ab in range(2):
-                x = agm[h, ab, :, :, here].reshape(64, 512)
+                x = agm[h, ab, :, :, here].reshape(64, 2048)
                 both = both + jnp.dot(sel_m[h, ab], x, preferred_element_type=F32)
-            sbm[h, :, :, here] = both.astype(BF16).reshape(4, 16, 512)
+            sbm[h, :, :, here] = both.astype(BF16).reshape(4, 16, 2048)
         w, dev = ws[h]
         m2[h] = [send(sbm.at[h, mod4(w + d)], rbm.at[h, d], dev[d]) for d in (1, 3, 2)]
 
@@ -229,6 +277,9 @@
     m_ua.wait_recv()
     products(zu, mate_core, 0)
 
+    merge(1)
+    merge(2)
+    merge(3)
     fw_a.wait_recv()
     m_oa = share(col(zo, core, 0), mate)
     fw_b.wait_recv()
@@ -237,23 +288,6 @@
     m_oa.wait_recv()
     m_ob.wait_recv()
     both_products(zo, mate_core)
-    cp_tab.wait()
-
-    def tile(n):
-        slot = n % 2
-        if n + 1 < TILES:
-            w_copy(n + 1, 1 - slot).start()
-        w_copy(n, slot).wait()
-
-        @pl.loop(0, CB)
-        def _(c):
-            for r in range(2):
-                k = stab[0, (n * 2 + r) * CB + c]
-                cols = pl.ds(pl.multiple_of(c * BS, BS), BS)
-                wbuf[slot, r * BS:(r + 1) * BS, cols] += dblk[k]
-
-        grad_out[:, pl.ds(n * TILE, TILE)] = lax.dot_general(
-            cbuf[...], wbuf[slot], (((1,), (1,)), ((), ())), preferred_element_type=F32).astype(BF16)
 
     def fill(h, quarter, chunk, ab):
         for e in range(2):
@@ -313,40 +347,19 @@
                 if d:
                     s2[h].append(send(r1.at[h, ch, e], ry2.at[h, d], wdev[d]))
 
-    cp_dr.wait()
-    rc = lax.broadcasted_iota(I32, (16, NBL), 0)
-    cc = lax.broadcasted_iota(I32, (16, NBL), 1)
-    my_row = cc == dp * 4 + (rc & 3)
-
-    @pl.loop(0, 8)
-    def _(j):
-        here = pl.ds(pl.multiple_of(j * 512, 512), 512)
-        rows = 0.0
-        for quarter in range(4):
-            there = pl.ds(pl.multiple_of(quarter * 4096 + j * 512, 512), 512)
-            pick = one_hot(my_row & ((rc >> 2) == quarter))
-            rows = rows + jnp.dot(pick, drow[:, there], preferred_element_type=F32)
-        cur[:, here] = rows
-
-
-    @pl.loop(0, BS)
-    def _(r):
-        dwide[pl.ds(r, NBL, stride=BS), :] = drow[:, pl.ds(pl.multiple_of(r * BS, BS), BS)].astype(F32)
-
-    @pl.loop(0, NBL)
-    def _(k):
-        dblk[k] = dwide[pl.ds(pl.multiple_of(k * BS, BS), BS), :].astype(BF16)
-
-    dblk[NBL] = jnp.zeros((BS, BS), BF16)
-
+    multiply(0)
+    multiply(1)
+    merge(4)
     combine(0)
-    tile(0)
+    multiply(2)
+    merge(5)
     combine(1)
-    tile(1)
+    multiply(3)
     second(0)
     second(1)
-    tile(2)
-    tile(3)
+    merge(6)
+    multiply(4)
+    multiply(5)
     for h in range(2):
         w, wdev = ws[h]
         for c in s2[h]:
@@ -402,16 +415,15 @@
         own = gath.at[h, w, u]
         d1[h] = [send(own, own, dev[d]) for d in (1, 3, 2)]
 
+    multiply(6)
+
     g2, d2 = [None, None], [None, None]
     for h in range(2):
         for c in g1[h]:
             c.wait_recv()
 
-        @pl.loop(0, 4)
-        def _(j):
-            here = pl.ds(pl.multiple_of(j * 512, 512), 512)
-            x = agg[h, :, :, here].reshape(64, 512)
-            sbg[h, :, :, here] = jnp.dot(sel_g[h], x, preferred_element_type=F32).astype(BF16).reshape(4, 32, 512)
+        sbg[h] = jnp.dot(
+            sel_g[h], agg[h].reshape(64, 2048), preferred_element_type=F32).astype(BF16).reshape(4, 32, 2048)
         w, dev = ws[h]
         g2[h] = [send(sbg.at[h, mod4(w + d)], rbg.at[h, d], dev[d]) for d in (2, 1, 3)]
     for h in range(2):
@@ -424,7 +436,6 @@
         w, dev = ws[h]
         lo, hi = gath.at[h, w, pl.ds(0, 2)], gath.at[h, w, pl.ds(2, 2)]
         d2[h] += [send(hi, hi, dev[1]), send(lo, lo, dev[3])]
-    tile(4)
     for h in range(2):
         w, dev = ws[h]
         d2[h][0].wait_recv()
@@ -434,7 +445,6 @@
         piece = gath.at[h, mod4(w + 1), pl.ds(2, 2)]
         f_dn = send(piece, piece, dev[3])
         d2[h] += [f_up, f_dn]
-    tile(5)
     for h in range(2):
         w, dev = ws[h]
         for c in g2[h]:
@@ -452,7 +462,6 @@
                 m, v = adam(got[quarter * 8:quarter * 8 + 8], m0, v0)
                 mnew[:, lanes] = jnp.where(filled, m, m0)
                 vnew[:, lanes] = jnp.where(filled, v, v0)
-    tile(6)
     for h in range(2):
         for c in d2[h][2:]:
             c.wait_recv()
@@ -475,13 +484,9 @@
         hit = ((rd & 63) == dev * 4 + (cd & 3)) & ((rd >> 6) == ((cd >> 2) & 3))
         sel[...] = jnp.where(hit, 1.0, 0.0).astype(BF16)
 
-        @pl.loop(0, 4)
-        def _(j):
-            x = gath[h, :, :, :, pl.ds(pl.multiple_of(j * 512, 512), 512)].reshape(256, 512)
-            y = jnp.dot(sel[...], x, preferred_element_type=F32).astype(BF16)
-            for quarter in range(4):
-                lanes = pl.ds(pl.multiple_of(quarter * 4096 + h * 2048 + j * 512, 512), 512)
-                dnew[:, lanes] = y[quarter * 64:(quarter + 1) * 64]
+        y = jnp.dot(sel[...], gath[h].reshape(256, 2048), preferred_element_type=F32).astype(BF16)
+        for quarter in range(4):
+            dnew[:, pl.ds(quarter * 4096 + h * 2048, 2048)] = y[quarter * 64:(quarter + 1) * 64]
         for quarter in range(4):
             lanes = pl.ds(quarter * 4096 + h * 2048, 2048)
             c = pltpu.make_async_copy(dnew.at[:, lanes], deltas_out.at[:, lanes], sem.at[6 + h * 4 + quarter])
@@ -510,7 +515,7 @@
             V((TOK, FFL), BF16),
             V((FFL, TOK), BF16),
             V((RB * CB, BS, BS), BF16),
-            V((2, TILE, D), BF16),
+            V((4, TILE, D), BF16),
             V((NBL, BS * BS), BF16),
             V((NBL * BS, BS), F32),
             V((NBL + 1, BS, BS), BF16),
@@ -536,7 +541,7 @@
             V((2, 2, 64, 64), BF16),
             V((2, 128, 64), BF16),
             pltpu.SemaphoreType.DMA((8,)),
-            pltpu.SemaphoreType.DMA((2,)),
+            pltpu.SemaphoreType.DMA((4,)),
             pltpu.SemaphoreType.DMA((N_REMOTE,)),
             pltpu.SemaphoreType.DMA((N_REMOTE,)),
         ],

time: 81.4 us -> 75.1 us (0.923)
  Pallas kernels: 80.3 us -> 74.2 us
    pallas_call x1, Pallas kernels: 77.3 us -> 71.8 us  [local(): pl.pallas_call(kernel, out_shape=(OUT((TOK, FFL), BF16), OUT((2, 4, 4, 16...]
where the time goes in v5:
time: 75.1 us; the launch traced here: 75 us
  Pallas kernels  74.2 us (99%)
  between operations  0.8 us (1%)
    pallas_call x1, Pallas kernels, local(): pl.pallas_call(kernel, out_shape=(OUT((TOK, FFL), BF16), OUT((2, 4, 4, 16...  71.8 us
    pallas_call x1, Pallas kernels, local(): pl.pallas_call(finish, out_shape=(jax.ShapeDtypeStruct((TOK, FFL), BF16),...  2.36 us

profile of v5, /device:TPU:0, one launch (start us, length us, event | category | flops | bytes accessed | tf_op | source)
XLA Modules:
  0.0 75.0 jit_solution(5863295510862429912)
XLA Ops:
  0.6 71.8 %shard_map.111 = (bf16[512,1792]{1,0:T(8,128)(2,1)S(1)}, bf16[2,4,4,16,2048]{4,3,2,1,0:T(8,128)(2,1)S(1)}, f32[8,16384]{1,0:T(8,128)S(1)}, f32[8,16384]{1,0:T(8,128)S(1)}) custom-call(bf16[512,512]{1,0:T(8,128)(2,1)} %cot.1, bf16[512,1792]{1,0:T(8,128)(2,1)} %hid.1, bf16[1792,4096]{1,0:T(8,128)(2,1)} %weight.1, bf16[64,16384]{1,0:T(8,128)(2,1)} %deltas.1, ...), custom_call_target="tpu_custom_call" | custom-call | flops 15000000512 | bytes 25000000 | tf_op jit(solution)/shard_map/pallas_call | solution.py:503
  72.4 2.4 %shard_map.112 = (bf16[512,1792]{1,0:T(8,128)(2,1)}, bf16[64,16384]{1,0:T(8,128)(2,1)}, f32[8,16384]{1,0:T(8,128)}, f32[8,16384]{1,0:T(8,128)}) custom-call(bf16[512,1792]{1,0:T(8,128)(2,1)S(1)} %get-tuple-element.12.grad, bf16[2,4,4,16,2048]{4,3,2,1,0:T(8,128)(2,1)S(1)} %get-tuple-element.13.gath, f32[8,16384]{1,0:T(8,128)S(1)} %get-tuple-element.14.mnew, ...), custom_call_target="tpu_custom_call" | custom-call | flops 500000000 | bytes 10000000 | tf_op jit(solution)/shard_map/pallas_call | solution.py:555

commit v6 on v5

--- a/solution.py
+++ b/solution.py
@@ -205,19 +205,6 @@
         cur[:, here] = rows
 
 
-    @pl.loop(0, BS // 8)
-    def _(rr):
-        for k in range(8):
-            r = rr * 8 + k
-            dwide[pl.ds(r, NBL, stride=BS), :] = drow[:, pl.ds(pl.multiple_of(r * BS, BS), BS)].astype(F32)
-
-    @pl.loop(0, NBL // 8)
-    def _(k):
-        at = pl.multiple_of(k * 8, 8)
-        dblk[pl.ds(at, 8)] = dwide[pl.ds(at * BS, 8 * BS), :].astype(BF16).reshape(8, BS, BS)
-
-    dblk[NBL] = jnp.zeros((BS, BS), BF16)
-
     def merge(n):
         slot = n % 4
         w_copy(n, slot).wait()
@@ -235,8 +222,6 @@
         if n + 4 < TILES:
             w_copy(n + 4, n % 4).start()
 
-    cp_tab.wait()
-    merge(0)
     up_a.wait_recv()
     fw_a = share(col(zd, core, 0), z_up)
     m_da = share(col(zd, core, 0), mate)
@@ -277,9 +262,7 @@
     m_ua.wait_recv()
     products(zu, mate_core, 0)
 
-    merge(1)
-    merge(2)
-    merge(3)
+    cp_tab.wait()
     fw_a.wait_recv()
     m_oa = share(col(zo, core, 0), mate)
     fw_b.wait_recv()
@@ -347,19 +330,31 @@
                 if d:
                     s2[h].append(send(r1.at[h, ch, e], ry2.at[h, d], wdev[d]))
 
+    @pl.loop(0, BS // 8)
+    def _(rr):
+        for k in range(8):
+            r = rr * 8 + k
+            dwide[pl.ds(r, NBL, stride=BS), :] = drow[:, pl.ds(pl.multiple_of(r * BS, BS), BS)].astype(F32)
+
+    @pl.loop(0, NBL // 8)
+    def _(k):
+        at = pl.multiple_of(k * 8, 8)
+        dblk[pl.ds(at, 8)] = dwide[pl.ds(at * BS, 8 * BS), :].astype(BF16).reshape(8, BS, BS)
+
+    dblk[NBL] = jnp.zeros((BS, BS), BF16)
+
+    combine(0)
+    merge(0)
+    merge(1)
     multiply(0)
+    combine(1)
+    merge(2)
     multiply(1)
-    merge(4)
-    combine(0)
-    multiply(2)
-    merge(5)
-    combine(1)
-    multiply(3)
     second(0)
     second(1)
-    merge(6)
-    multiply(4)
-    multiply(5)
+    merge(3)
+    multiply(2)
+    multiply(3)
     for h in range(2):
         w, wdev = ws[h]
         for c in s2[h]:
@@ -415,8 +410,6 @@
         own = gath.at[h, w, u]
         d1[h] = [send(own, own, dev[d]) for d in (1, 3, 2)]
 
-    multiply(6)
-
     g2, d2 = [None, None], [None, None]
     for h in range(2):
         for c in g1[h]:
@@ -436,15 +429,9 @@
         w, dev = ws[h]
         lo, hi = gath.at[h, w, pl.ds(0, 2)], gath.at[h, w, pl.ds(2, 2)]
         d2[h] += [send(hi, hi, dev[1]), send(lo, lo, dev[3])]
-    for h in range(2):
-        w, dev = ws[h]
-        d2[h][0].wait_recv()
-        piece = gath.at[h, mod4(w - 1), pl.ds(0, 2)]
-        f_up = send(piece, piece, dev[1])
-        d2[h][1].wait_recv()
-        piece = gath.at[h, mod4(w + 1), pl.ds(2, 2)]
-        f_dn = send(piece, piece, dev[3])
-        d2[h] += [f_up, f_dn]
+    for n in range(4, TILES):
+        merge(n)
+        multiply(n)
     for h in range(2):
         w, dev = ws[h]
         for c in g2[h]:
@@ -462,6 +449,15 @@
                 m, v = adam(got[quarter * 8:quarter * 8 + 8], m0, v0)
                 mnew[:, lanes] = jnp.where(filled, m, m0)
                 vnew[:, lanes] = jnp.where(filled, v, v0)
+    for h in range(2):
+        w, dev = ws[h]
+        d2[h][0].wait_recv()
+        piece = gath.at[h, mod4(w - 1), pl.ds(0, 2)]
+        f_up = send(piece, piece, dev[1])
+        d2[h][1].wait_recv()
+        piece = gath.at[h, mod4(w + 1), pl.ds(2, 2)]
+        f_dn = send(piece, piece, dev[3])
+        d2[h] += [f_up, f_dn]
     for h in range(2):
         for c in d2[h][2:]:
             c.wait_recv()

time: 75.1 us -> 72.9 us (0.971)
  Pallas kernels: 74.2 us -> 71.6 us
    pallas_call x1, Pallas kernels: 71.8 us -> 69.3 us  [local(): pl.pallas_call(kernel, out_shape=(OUT((TOK, FFL), BF16), OUT((2, 4, 4, 16...]
where the time goes in v6:
time: 72.9 us; the launch traced here: 72.4 us
  Pallas kernels  71.6 us (98%)
  between operations  0.8 us (1%)
    pallas_call x1, Pallas kernels, local(): pl.pallas_call(kernel, out_shape=(OUT((TOK, FFL), BF16), OUT((2, 4, 4, 16...  69.3 us
    pallas_call x1, Pallas kernels, local(): pl.pallas_call(finish, out_shape=(jax.ShapeDtypeStruct((TOK, FFL), BF16),...  2.36 us

profile of v6, /device:TPU:0, one launch (start us, length us, event | category | flops | bytes accessed | tf_op | source)
XLA Modules:
  0.0 72.4 jit_solution(15826119233242667164)
XLA Ops:
  0.6 69.3 %shard_map.111 = (bf16[512,1792]{1,0:T(8,128)(2,1)S(1)}, bf16[2,4,4,16,2048]{4,3,2,1,0:T(8,128)(2,1)S(1)}, f32[8,16384]{1,0:T(8,128)S(1)}, f32[8,16384]{1,0:T(8,128)S(1)}) custom-call(bf16[512,512]{1,0:T(8,128)(2,1)} %cot.1, bf16[512,1792]{1,0:T(8,128)(2,1)} %hid.1, bf16[1792,4096]{1,0:T(8,128)(2,1)} %weight.1, bf16[64,16384]{1,0:T(8,128)(2,1)} %deltas.1, ...), custom_call_target="tpu_custom_call" | custom-call | flops 15000000512 | bytes 25000000 | tf_op jit(solution)/shard_map/pallas_call | solution.py:499
  69.9 2.4 %shard_map.112 = (bf16[512,1792]{1,0:T(8,128)(2,1)}, bf16[64,16384]{1,0:T(8,128)(2,1)}, f32[8,16384]{1,0:T(8,128)}, f32[8,16384]{1,0:T(8,128)}) custom-call(bf16[512,1792]{1,0:T(8,128)(2,1)S(1)} %get-tuple-element.12.grad, bf16[2,4,4,16,2048]{4,3,2,1,0:T(8,128)(2,1)S(1)} %get-tuple-element.13.gath, f32[8,16384]{1,0:T(8,128)S(1)} %get-tuple-element.14.mnew, ...), custom_call_target="tpu_custom_call" | custom-call | flops 500000000 | bytes 10000000 | tf_op jit(solution)/shard_map/pallas_call | solution.py:551

commit v7 on v6

--- a/solution.py
+++ b/solution.py
@@ -29,7 +29,7 @@
 
 MESH = pl.DeviceIdType.MESH
 BF16, F32, I32 = jnp.bfloat16, jnp.float32, jnp.int32
-N_REMOTE = 96
+N_REMOTE = 128
 VMEM_MAIN = 56 * 1024 * 1024
 OUT = pltpu.VMEM
 
@@ -42,7 +42,7 @@
     cot, hid, weight, deltas, ids_row, own_row, first, second,
     grad_out, gath, mnew, vnew,
     cbuf, hbuf, ht, dense, wbuf, drow, dwide, dblk, stage, rx, ry, cb, r1, ry2, gsum,
-    agm, sbm, rbm, agg, sbg, rbg, g16, cur, mbuf, vbuf, tab, stab,
+    agm, sbm, rbm, agg, sbg, rbg, rxg, cbg, g16, cur, mbuf, vbuf, tab, stab,
     sel_m, sel_g, lsem, wsem, ssem, rsem,
 ):
     dp, mp = lax.axis_index("dp"), lax.axis_index("mp")
@@ -418,7 +418,10 @@
         sbg[h] = jnp.dot(
             sel_g[h], agg[h].reshape(64, 2048), preferred_element_type=F32).astype(BF16).reshape(4, 32, 2048)
         w, dev = ws[h]
-        g2[h] = [send(sbg.at[h, mod4(w + d)], rbg.at[h, d], dev[d]) for d in (2, 1, 3)]
+        opp, qu, qd = mod4(w + 2), mod4(w + 1), mod4(w - 1)
+        lo, hi = pl.ds(0, 16), pl.ds(16, 16)
+        g2[h] = [send(sbg.at[h, opp, lo], rxg.at[h, 0], dev[1]), send(sbg.at[h, opp, hi], rxg.at[h, 1], dev[3]),
+                 send(sbg.at[h, qu, hi], rbg.at[h, 0, hi], dev[1]), send(sbg.at[h, qd, lo], rbg.at[h, 1, lo], dev[3])]
     for h in range(2):
         w, dev = ws[h]
         for c in d1[h]:
@@ -429,19 +432,38 @@
         w, dev = ws[h]
         lo, hi = gath.at[h, w, pl.ds(0, 2)], gath.at[h, w, pl.ds(2, 2)]
         d2[h] += [send(hi, hi, dev[1]), send(lo, lo, dev[3])]
-    for n in range(4, TILES):
-        merge(n)
-        multiply(n)
-    for h in range(2):
-        w, dev = ws[h]
-        for c in g2[h]:
+    merge(4)
+    multiply(4)
+    for h in range(2):
+        w, dev = ws[h]
+        for ab, q, d in ((0, mod4(w + 1), 1), (1, mod4(w - 1), 3)):
+            g2[h][ab].wait_recv()
+            part = slice(ab * 16, ab * 16 + 16)
+            cbg[h, ab] = sbg[h, q, part] + rxg[h, ab]
+            g2[h].append(send(cbg.at[h, ab], rbg.at[h, ab, part], dev[d]))
+    merge(5)
+    multiply(5)
+    merge(6)
+    multiply(6)
+    for h in range(2):
+        w, dev = ws[h]
+        d2[h][0].wait_recv()
+        piece = gath.at[h, mod4(w - 1), pl.ds(0, 2)]
+        f_up = send(piece, piece, dev[1])
+        d2[h][1].wait_recv()
+        piece = gath.at[h, mod4(w + 1), pl.ds(2, 2)]
+        f_dn = send(piece, piece, dev[3])
+        d2[h] += [f_up, f_dn]
+    for h in range(2):
+        w, dev = ws[h]
+        for c in g2[h][2:]:
             c.wait_recv()
 
         @pl.loop(0, 4)
         def _(j):
             here = pl.ds(pl.multiple_of(j * 512, 512), 512)
             got = sbg[h, w, :, here].astype(F32)
-            for d in (1, 2, 3):
+            for d in range(2):
                 got = got + rbg[h, d, :, here].astype(F32)
             for quarter in range(4):
                 lanes = pl.ds(pl.multiple_of(quarter * 4096 + h * 2048 + j * 512, 512), 512)
@@ -449,15 +471,6 @@
                 m, v = adam(got[quarter * 8:quarter * 8 + 8], m0, v0)
                 mnew[:, lanes] = jnp.where(filled, m, m0)
                 vnew[:, lanes] = jnp.where(filled, v, v0)
-    for h in range(2):
-        w, dev = ws[h]
-        d2[h][0].wait_recv()
-        piece = gath.at[h, mod4(w - 1), pl.ds(0, 2)]
-        f_up = send(piece, piece, dev[1])
-        d2[h][1].wait_recv()
-        piece = gath.at[h, mod4(w + 1), pl.ds(2, 2)]
-        f_dn = send(piece, piece, dev[3])
-        d2[h] += [f_up, f_dn]
     for h in range(2):
         for c in d2[h][2:]:
             c.wait_recv()
@@ -527,7 +540,9 @@
             V((2, 4, 16, 4096), BF16),
             V((2, 4, 16, 2048), BF16),
             V((2, 4, 32, 2048), BF16),
-            V((2, 4, 32, 2048), BF16),
+            V((2, 2, 32, 2048), BF16),
+            V((2, 2, 16, 2048), BF16),
+            V((2, 2, 16, 2048), BF16),
             V((16, 4096), F32),
             V((16, 4096), F32),
             V((CAP, BS * BS), F32),

time: 72.9 us -> 72.7 us (level)
  no operation moved by 1% of the time
where the time goes in v7:
time: 72.7 us; the launch traced here: 72.6 us
  Pallas kernels  71.8 us (99%)
  between operations  0.8 us (1%)
    pallas_call x1, Pallas kernels, local(): pl.pallas_call(kernel, out_shape=(OUT((TOK, FFL), BF16), OUT((2, 4, 4, 16...  69.4 us
    pallas_call x1, Pallas kernels, local(): pl.pallas_call(finish, out_shape=(jax.ShapeDtypeStruct((TOK, FFL), BF16),...  2.36 us

profile of v7, /device:TPU:0, one launch (start us, length us, event | category | flops | bytes accessed | tf_op | source)
XLA Modules:
  0.0 72.6 jit_solution(6732315903282291406)
XLA Ops:
  0.6 69.4 %shard_map.111 = (bf16[512,1792]{1,0:T(8,128)(2,1)S(1)}, bf16[2,4,4,16,2048]{4,3,2,1,0:T(8,128)(2,1)S(1)}, f32[8,16384]{1,0:T(8,128)S(1)}, f32[8,16384]{1,0:T(8,128)S(1)}) custom-call(bf16[512,512]{1,0:T(8,128)(2,1)} %cot.1, bf16[512,1792]{1,0:T(8,128)(2,1)} %hid.1, bf16[1792,4096]{1,0:T(8,128)(2,1)} %weight.1, bf16[64,16384]{1,0:T(8,128)(2,1)} %deltas.1, ...), custom_call_target="tpu_custom_call" | custom-call | flops 15000000512 | bytes 25000000 | tf_op jit(solution)/shard_map/pallas_call | solution.py:512
  70.1 2.4 %shard_map.112 = (bf16[512,1792]{1,0:T(8,128)(2,1)}, bf16[64,16384]{1,0:T(8,128)(2,1)}, f32[8,16384]{1,0:T(8,128)}, f32[8,16384]{1,0:T(8,128)}) custom-call(bf16[512,1792]{1,0:T(8,128)(2,1)S(1)} %get-tuple-element.12.grad, bf16[2,4,4,16,2048]{4,3,2,1,0:T(8,128)(2,1)S(1)} %get-tuple-element.13.gath, f32[8,16384]{1,0:T(8,128)S(1)} %get-tuple-element.14.mnew, ...), custom_call_target="tpu_custom_call" | custom-call | flops 500000000 | bytes 10000000 | tf_op jit(solution)/shard_map/pallas_call | solution.py:566
